TPU v7x, 32 devices: a whole 2x2x4 slice. The times are simulated.
32 devices in a mesh: ctx: 8 (over z, x), tp: 4 (over y, core).
Axes of the slice: x: 2, y: 2, z: 4, core: 2. Of those that a mesh axis runs over, the one named last changes fastest.
Arguments:
- signal: bfloat16 [4096, 2048], P('tp', 'ctx'), may hold values from -6 to 6
- pre_gate: bfloat16 [4096, 2048], P('tp', 'ctx'), may hold values from -6 to 6
- post_gate: bfloat16 [4096, 2048], P('tp', 'ctx'), may hold values from -6 to 6
- filter_taps: float32 [4096, 2048], P('tp', 'ctx'), may hold values from -0.125 to 0.125
- skip_gain: float32 [4096], P('tp'), may hold values from -4 to 4
- out_weight: bfloat16 [4096, 4096], P('tp'), may hold values from -0.125 to 0.125
Outputs:
- projected: bfloat16 [4096, 2048], P('tp', 'ctx')
All inputs are finite; a program needn't handle non-finite values.
Results may differ from a plain program's by a relative error of at most 0.027.
Values may be sent and summed in bfloat16 or wider, within the bound.
A program may use at most 64 MiB of HBM per device.

v0:
```python
import math

import jax
import jax.numpy as jnp
from jax import lax
from jax.sharding import PartitionSpec as P

highest = lax.Precision.HIGHEST
two_pi = 2.0 * math.pi


def shortened(shard):

    def short(part):
        return part.astype(jnp.bfloat16) if part.dtype == jnp.float32 else part

    return jax.tree.map(short, shard)


def angle_tables(count, period):
    first = jnp.arange(count, dtype=jnp.int32)
    second = jnp.arange(period, dtype=jnp.int32)
    angle = (first[:, None] * second[None, :] % period).astype(jnp.float32) * (two_pi / period)
    return (jnp.cos(angle), jnp.sin(angle))


def twiddle_tables(freq_first, freq_count, tokens_here, total_len):
    freq = freq_first + jnp.arange(freq_count, dtype=jnp.int32)
    place = jnp.arange(tokens_here, dtype=jnp.int32)
    angle = (freq[:, None] * place[None, :] % total_len).astype(jnp.float32) * (two_pi / total_len)
    return (jnp.cos(angle), jnp.sin(angle))


def matmul_high(left, right):
    return jnp.matmul(left, right, precision=highest)


def front_section(blocks, devices):
    cosine, sine = angle_tables(devices, 2 * devices)
    real_part = jnp.einsum("scan,ak->sckn", blocks, cosine, precision=highest)
    imag_part = -jnp.einsum("scan,ak->sckn", blocks, sine, precision=highest)
    return jnp.stack([real_part, imag_part])


def middle_section(spectrum, freq_first, total_len):
    tokens_here = spectrum.shape[-1]
    twid_cos, twid_sin = twiddle_tables(freq_first, spectrum.shape[3], tokens_here, total_len)
    turned_real = spectrum[0] * twid_cos + spectrum[1] * twid_sin
    turned_imag = spectrum[1] * twid_cos - spectrum[0] * twid_sin
    square_cos, square_sin = angle_tables(tokens_here, tokens_here)
    full_real = matmul_high(turned_real, square_cos) + matmul_high(turned_imag, square_sin)
    full_imag = matmul_high(turned_imag, square_cos) - matmul_high(turned_real, square_sin)
    prod_real = full_real[0] * full_real[1] - full_imag[0] * full_imag[1]
    prod_imag = full_real[0] * full_imag[1] + full_imag[0] * full_real[1]
    back_real = matmul_high(prod_real, square_cos) - matmul_high(prod_imag, square_sin)
    back_imag = matmul_high(prod_imag, square_cos) + matmul_high(prod_real, square_sin)
    out_real = back_real * twid_cos - back_imag * twid_sin
    out_imag = back_real * twid_sin + back_imag * twid_cos
    return jnp.stack([out_real, out_imag])


def back_section(wide, devices, total_len):
    cosine, sine = angle_tables(devices, 2 * devices)
    summed = jnp.einsum("ckn,ak->can", wide[0], cosine, precision=highest)
    summed = summed - jnp.einsum("ckn,ak->can", wide[1], sine, precision=highest)
    return summed * (1.0 / total_len)


def per_device(signal, pre_gate, post_gate, filter_taps, skip_gain, out_weight):
    channels_here, tokens_here = signal.shape
    devices = lax.axis_size("ctx")
    total_len = 2 * devices * tokens_here
    gated_input = signal.astype(jnp.float32) * pre_gate.astype(jnp.float32)
    stacked = jnp.stack([gated_input, filter_taps])[:, :, None, :]
    blocks = lax.all_to_all(
        stacked.astype(jnp.bfloat16), "ctx", split_axis=3, concat_axis=2, tiled=True
    ).astype(stacked.dtype)
    spectrum = lax.all_to_all(
        front_section(blocks, devices).astype(jnp.bfloat16),
        "ctx",
        split_axis=3,
        concat_axis=4,
        tiled=True,
    ).astype(jnp.float32)
    freq_first = lax.axis_index("ctx") * spectrum.shape[3]
    wide = middle_section(spectrum, freq_first, total_len)
    regathered = lax.all_to_all(
        shortened(wide), "ctx", split_axis=3, concat_axis=2, tiled=True
    ).astype(wide.dtype)
    convolved = lax.all_to_all(
        shortened(back_section(regathered, devices, total_len)),
        "ctx",
        split_axis=1,
        concat_axis=2,
        tiled=True,
    )[:, 0, :]
    mixed = (post_gate.astype(jnp.float32) * (convolved + skip_gain[:, None] * gated_input)).astype(
        jnp.bfloat16
    )
    return lax.psum_scatter(
        lax.dot_general(
            out_weight, mixed, (((0,), (0,)), ((), ())), preferred_element_type=jnp.float32
        ).astype(jnp.bfloat16),
        "tp",
        scatter_dimension=0,
        tiled=True,
    )


def solution(mesh):
    return jax.shard_map(
        per_device,
        mesh=mesh,
        in_specs=(
            P("tp", "ctx"),
            P("tp", "ctx"),
            P("tp", "ctx"),
            P("tp", "ctx"),
            P("tp"),
            P("tp", None),
        ),
        out_specs=P("tp", "ctx"),
        check_vma=False,
    )
```

profile of v0, /device:TPU:0, one launch (start us, length us, event | category | flops | bytes accessed | tf_op | source)
XLA Modules:
  0.0 334.6 jit_solution(15326724648898506773)
XLA Ops:
  6.5 1.2 copy.48
  7.8 1.4 copy.49
  9.2 1.6 copy.50
  10.9 0.2 fusion.28
  11.1 0.1 pad_maximum_fusion.2
  11.2 1.1 copy.51
  12.3 32.8 %all_to_all.45 = bf16[2,1024,1,256]{1,0,2,3:T(2,128)(2,1)S(1)} all-to-all(bf16[2,1024,1,256]{1,0,2,3:T(2,128)(2,1)S(1)} %copy.51), channel_id=1, replica_groups=mesh['ctx'=8,'tp'=4] {'ctx'}, dimensions={3} | all-to-all | bytes 2097152 | tf_op jit(solution)/shard_map/all_to_all | solution.py:75
  45.1 0.3 copy.52
  45.4 2.2 convert_bitcast_fusion.1
  47.6 2.2 fusion.9
  49.8 0.4 pad_maximum_fusion
  50.2 4.3 %copy.55 = bf16[2,2,1024,16,32]{2,4,1,0,3:T(8,128)(2,1)} copy(bf16[2,2,1024,16,32]{2,3,4,1,0:T(8,128)(2,1)S(1)} %pad_maximum_fusion) | data formatting | bytes 8388608 | tf_op jit(solution)/shard_map/stack | solution.py:42
  54.5 4.8 %all-to-all-start.1 = ((bf16[2,2,1024,16,32]{2,4,1,0,3:T(8,128)(2,1)}), bf16[2,2,1024,16,32]{2,4,1,0,3:T(8,128)(2,1)}, u32[]{:S(2)}, u32[]{:S(2)}) async-start(bf16[2,2,1024,16,32]{2,4,1,0,3:T(8,128)(2,1)} %copy.55), calls=%async_computation.1 | async-start | bytes 8388608 | tf_op jit(solution)/shard_map/all_to_all | solution.py:78
  59.3 0.1 fusion.76
  59.5 92.0 %all-to-all-done.1 = bf16[2,2,1024,16,32]{2,4,1,0,3:T(8,128)(2,1)} async-done(((bf16[2,2,1024,16,32]{2,4,1,0,3:T(8,128)(2,1)}), bf16[2,2,1024,16,32]{2,4,1,0,3:T(8,128)(2,1)}, u32[]{:S(2)}, u32[]{:S(2)}) %all-to-all-start.1) | async-done | bytes 4194336 | tf_op jit(solution)/shard_map/all_to_all | solution.py:78
  151.4 2.6 copy.56
  154.0 1.0 convert_bitcast_fusion
  155.1 1.7 fusion.125
  156.8 0.3 copy.57
  157.1 0.3 copy.58
  157.4 8.5 %fusion.17 = f32[2,1024,2,256]{3,1,2,0:T(8,128)S(1)} fusion(f32[2,1024,2,256]{1,3,2,0:T(8,128)S(1)} %bitcast.102, f32[2,1024,2,256]{1,3,2,0:T(8,128)S(1)} %bitcast.98, f32[2,256]{1,0:T(2,128)S(1)} %get-tuple-element.14, f32[2,256]{1,0:T(2,128)S(1)} %get-tuple-element.13), kind=kOutput, calls=%fused_computation.28 | convolution fusion | flops 3225288704 | bytes 12587008 | tf_op jit(solution)/shard_map/dot_general | solution.py:35
  165.9 8.9 %fusion.18 = f32[2,1024,2,256]{3,1,2,0:T(8,128)S(1)} fusion(f32[2,1024,2,256]{1,3,2,0:T(8,128)S(1)} %bitcast.99, f32[2,1024,2,256]{1,3,2,0:T(8,128)S(1)} %bitcast.103, f32[2,256]{1,0:T(2,128)S(1)} %get-tuple-element.14, f32[2,256]{1,0:T(2,128)S(1)} %get-tuple-element.13), kind=kOutput, calls=%fused_computation.29 | convolution fusion | flops 3225288704 | bytes 12587008 | tf_op jit(solution)/shard_map/dot_general | solution.py:35
  174.7 8.7 %convolution_add_fusion = f32[2,1024,2,256]{3,1,2,0:T(8,128)S(1)} fusion(f32[2,1024,2,256]{3,1,2,0:T(8,128)S(1)} %fusion.17, f32[2,1024,2,256]{1,3,2,0:T(8,128)S(1)} %bitcast.100, f32[2,1024,2,256]{1,3,2,0:T(8,128)S(1)} %bitcast.104, f32[2,256]{1,0:T(2,128)S(1)} %get-tuple-element.14, f32[2,256]{1,0:T(2,128)S(1)} %get-tuple-element.13), kind=kOutput, calls=%fused_computation.8 | convolution fusion | flops 3226337280 | bytes 16781312 | tf_op jit(solution)/shard_map/dot_general | solution.py:35
  183.4 8.5 %convolution_subtract_fusion = f32[2,1024,2,256]{3,1,2,0:T(8,128)S(1)} fusion(f32[2,1024,2,256]{3,1,2,0:T(8,128)S(1)} %fusion.18, f32[2,1024,2,256]{1,3,2,0:T(8,128)S(1)} %bitcast.105, f32[2,1024,2,256]{1,3,2,0:T(8,128)S(1)} %bitcast.101, f32[2,256]{1,0:T(2,128)S(1)} %get-tuple-element.14, f32[2,256]{1,0:T(2,128)S(1)} %get-tuple-element.13), kind=kOutput, calls=%fused_computation.7 | convolution fusion | flops 3226337280 | bytes 16781312 | tf_op jit(solution)/shard_map/dot_general | solution.py:35
  192.0 0.5 multiply_subtract_fusion.1
  192.5 3.1 fusion.3
  195.6 2.8 fusion.1
  198.4 2.9 fusion.10
  201.4 3.2 fusion.21
  204.6 0.2 pad_maximum_fusion.1
  204.8 4.3 %copy.63 = bf16[2,1024,2,256]{1,2,0,3:T(2,128)(2,1)} copy(bf16[2,1024,2,256]{3,1,2,0:T(8,128)(2,1)S(1)} %pad_maximum_fusion.1) | data formatting | bytes 4194304 | tf_op jit(solution)/shard_map/stack | solution.py:59
  209.1 52.0 %all_to_all.46 = bf16[2,1024,2,256]{1,2,0,3:T(2,128)(2,1)S(1)} all-to-all(bf16[2,1024,2,256]{1,2,0,3:T(2,128)(2,1)} %copy.63), channel_id=1, replica_groups=mesh['ctx'=8,'tp'=4] {'ctx'}, dimensions={3} | all-to-all | bytes 4194304 | tf_op jit(solution)/shard_map/all_to_all | solution.py:87
  261.1 0.6 copy.64
  261.8 1.2 fusion.126
  262.9 1.1 copy.65
  264.0 0.4 squeeze.10
  264.5 0.6 fusion.61
  265.1 2.3 copy.66
  267.4 0.4 squeeze.11
  267.9 0.6 fusion.20
  268.5 1.1 copy.67
  269.6 3.6 %all-to-all-start.3 = ((bf16[1024,8,32]{0,2,1:T(8,128)(2,1)}), bf16[1024,8,32]{0,2,1:T(8,128)(2,1)S(1)}, u32[]{:S(2)}, u32[]{:S(2)}) async-start(bf16[1024,8,32]{0,2,1:T(8,128)(2,1)} %copy.67), calls=%async_computation.3 | async-start | bytes 1048576 | tf_op jit(solution)/shard_map/all_to_all | solution.py:90
  273.2 0.0 reduce-scatter.2.cloned.1.call-start
  273.3 1.2 copy.47
  274.5 12.9 %all-to-all-done.3 = bf16[1024,8,32]{0,2,1:T(8,128)(2,1)S(1)} async-done(((bf16[1024,8,32]{0,2,1:T(8,128)(2,1)}), bf16[1024,8,32]{0,2,1:T(8,128)(2,1)S(1)}, u32[]{:S(2)}, u32[]{:S(2)}) %all-to-all-start.3) | async-done | bytes 524320 | tf_op jit(solution)/shard_map/all_to_all | solution.py:90
  287.4 7.1 %fusion = bf16[4096,256]{0,1:T(8,128)(2,1)} fusion(bf16[1024,4096]{1,0:T(8,128)(2,1)} %param.11, bf16[1024,256]{0,1:T(8,128)(2,1)S(1)} %bitcast.111, bf16[1024,256]{0,1:T(8,128)(2,1)S(1)} %copy.47, bf16[1024,256]{0,1:T(8,128)(2,1)S(1)} %copy-done.3, bf16[1024,256]{0,1:T(8,128)(2,1)S(1)} %copy-done.1, f32[1024]{0:T(1024)S(1)} %copy-done.4), kind=kOutput, calls=%fused_computation.2 | convolution fusion | flops 2150891520 | bytes 12587008 | tf_op jit(solution)/shard_map/dot_general | solution.py:101
  294.6 30.7 %reduce-scatter.2.cloned.1.call-done = bf16[1024,256]{0,1:T(8,128)(2,1)} async-done(((bf16[4096,256]{0,1:T(8,128)(2,1)}), bf16[1024,256]{0,1:T(8,128)(2,1)}) %reduce-scatter.2.cloned.1.call-update) | async-done | bytes 524304 | tf_op jit(solution)/shard_map/reduce_scatter | solution.py:100
  325.3 2.0 copy.68
  (12 shorter events, 0.0 us)
Async XLA Ops:
  7.8 4.5 %copy-start = (bf16[1024,256]{0,1:T(8,128)(2,1)}, bf16[1024,256]{0,1:T(8,128)(2,1)S(1)}, u32[]{:S(2)}) copy-start(bf16[1024,256]{0,1:T(8,128)(2,1)S(1)} %copy.48) | copy-start | bytes 1572868
  9.2 35.9 %copy-start.2 = (bf16[1024,256]{0,1:T(8,128)(2,1)}, bf16[1024,256]{0,1:T(8,128)(2,1)S(1)}, u32[]{:S(2)}) copy-start(bf16[1024,256]{0,1:T(8,128)(2,1)S(1)} %copy.49) | copy-start | bytes 1572868
  54.5 96.9 %all-to-all-start.1 = ((bf16[2,2,1024,16,32]{2,4,1,0,3:T(8,128)(2,1)}), bf16[2,2,1024,16,32]{2,4,1,0,3:T(8,128)(2,1)}, u32[]{:S(2)}, u32[]{:S(2)}) async-start(bf16[2,2,1024,16,32]{2,4,1,0,3:T(8,128)(2,1)} %copy.55), calls=%async_computation.1 | async-start | bytes 8388608 | tf_op jit(solution)/shard_map/all_to_all | solution.py:78
  267.4 20.0 %copy-start.4 = (f32[1024]{0:T(1024)S(1)}, f32[1024]{0:T(1024)}, u32[]{:S(2)}) copy-start(f32[1024]{0:T(1024)} %param.10) | copy-start | bytes 12292
  267.9 19.6 %copy-start.1 = (bf16[1024,256]{0,1:T(8,128)(2,1)S(1)}, bf16[1024,256]{0,1:T(8,128)(2,1)}, u32[]{:S(2)}) copy-start(bf16[1024,256]{0,1:T(8,128)(2,1)} %copy-done) | copy-start | bytes 1572868
  267.9 19.6 %copy-start.3 = (bf16[1024,256]{0,1:T(8,128)(2,1)S(1)}, bf16[1024,256]{0,1:T(8,128)(2,1)}, u32[]{:S(2)}) copy-start(bf16[1024,256]{0,1:T(8,128)(2,1)} %copy-done.2) | copy-start | bytes 1572868
  269.6 17.8 %all-to-all-start.3 = ((bf16[1024,8,32]{0,2,1:T(8,128)(2,1)}), bf16[1024,8,32]{0,2,1:T(8,128)(2,1)S(1)}, u32[]{:S(2)}, u32[]{:S(2)}) async-start(bf16[1024,8,32]{0,2,1:T(8,128)(2,1)} %copy.67), calls=%async_computation.3 | async-start | bytes 1048576 | tf_op jit(solution)/shard_map/all_to_all | solution.py:90
  273.2 52.0 %reduce-scatter.2.cloned.1.call-start = ((), (), s32[]{:S(2)}) async-start(), calls=%async_computation.5 | async-start | bytes 2621440 | tf_op jit(solution)/shard_map/reduce_scatter | solution.py:100
Sparse Core Ops, SparseCore 0:
  294.7 30.5 reduce-scatter.1
where the time goes:
time: 341 us; the launch traced here: 335 us
  waiting for transfers between devices  136 us (40%)
  blocking collectives  84.8 us (25%)
  matrix products  59.4 us (17%)
  local copies, waits for them, and re-layouts  29.7 us (9%)
  between operations  14.1 us (4%)
  starting transfers between devices  8.43 us (2%)
    all_to_all x1, waiting for transfers between devices, per_device(): lax.all_to_all(front_section(blocks, devices).astype(jnp.bfloat16), 'ctx'...  92 us
    all_to_all x1, blocking collectives, per_device(): lax.all_to_all(shortened(wide), 'ctx', split_axis=3, concat_axis=2, tiled...  52 us
    dot_general x8, matrix products, matmul_high(): return jnp.matmul(left, right, precision=highest)  46.6 us
    all_to_all x1, blocking collectives, per_device(): lax.all_to_all(stacked.astype(jnp.bfloat16), 'ctx', split_axis=3, concat_...  32.8 us
    reduce_scatter x1, waiting for transfers between devices, per_device(): lax.psum_scatter(lax.dot_general(out_weight, mixed, (((0,), (0,)), ((), (...  30.7 us
    all_to_all x1, waiting for transfers between devices, per_device(): lax.all_to_all(shortened(back_section(regathered, devices, total_len)), '...  12.9 us
    dot_general x1, matrix products, per_device(): lax.dot_general(out_weight, mixed, (((0,), (0,)), ((), ())), preferred_el...  7.13 us
  transfers between devices with their start and end apart: 3, of which 3 were waited for; matrix products, arithmetic and copies ran while one was open for 0% of the time, Pallas kernels for 0%

commit v1 on v0

v1 whole, which is shorter than its diff:
```python
import functools
import math

import jax
import jax.numpy as jnp
import numpy as np
from jax import lax
from jax.experimental import pallas as pl
from jax.experimental.pallas import tpu as pltpu
from jax.sharding import PartitionSpec as P

f32 = jnp.float32
bf16 = jnp.bfloat16


def freq_tables(blocks, width):
    total = 2 * blocks * width
    place = np.arange(width, dtype=np.int64)
    tables = []
    for k1 in range(blocks + 1):
        angle = (place[:, None] * (k1 + 2 * blocks * place[None, :]) % total) * (2.0 * math.pi / total)
        c, s = np.cos(angle), np.sin(angle)
        tables.append(np.block([[c, -s], [s, c]]))
    return np.stack(tables).astype(jnp.bfloat16)


def weighted(terms):
    total = None
    for coef, part in terms:
        if abs(coef) < 1e-12:
            continue
        value = part if coef == 1.0 else (-part if coef == -1.0 else part * coef)
        total = value if total is None else total + value
    return total


def unit(fn, b, k1, n):
    value = fn(math.pi * (b * k1 % (2 * n)) / n)
    return float(round(value)) if abs(value - round(value)) < 1e-12 else value


def front(n, rows, load, spec):
    width = spec.shape[-1] // 2
    x = [load(b) for b in range(n)]
    even, odd = range(0, n, 2), range(1, n, 2)
    for k1 in range(n // 2 + 1):
        ce = weighted([(unit(math.cos, b, k1, n), x[b]) for b in even])
        co = weighted([(unit(math.cos, b, k1, n), x[b]) for b in odd])
        se = weighted([(unit(math.sin, b, k1, n), x[b]) for b in even])
        so = weighted([(unit(math.sin, b, k1, n), x[b]) for b in odd])
        k2 = n - k1
        if k1 == k2:
            spec[k1, rows, :width] = ce.astype(bf16)
            spec[k1, rows, width:] = (-so).astype(bf16)
            continue
        spec[k1, rows, :width] = (ce + co).astype(bf16)
        spec[k2, rows, :width] = (ce - co).astype(bf16)
        if k1:
            spec[k1, rows, width:] = (-(se + so)).astype(bf16)
            spec[k2, rows, width:] = (se - so).astype(bf16)


def middle(k1, channels, real_only, spec, table, wide):
    width = table.shape[-1] // 2
    depth = width if real_only else 2 * width
    full = jnp.dot(spec[k1, :, :depth], table[k1, :depth, :], preferred_element_type=f32)
    ur, ui = full[:channels, :width], full[:channels, width:]
    hr, hi = full[channels:, :width], full[channels:, width:]
    prod = jnp.concatenate([ur * hr - ui * hi, ur * hi + ui * hr], axis=1).astype(bf16)
    wide[k1, :, :depth] = lax.dot_general(
        prod, table[k1, :depth, :], (((1,), (1,)), ((), ())), preferred_element_type=f32
    )


def back(n, rows, wide, store):
    width = wide.shape[-1] // 2
    scale = 1.0 / (2 * n * width)
    re = [wide[k, rows, :width] for k in range(n + 1)]
    im = [None if k in (0, n) else wide[k, rows, width:] for k in range(n + 1)]
    for parity in (0, 1):
        sign = 1.0 if parity == 0 else -1.0
        reals, imags = [], []
        for k in range(n // 2):
            reals.append(re[k] + re[n - k] if parity == 0 else re[k] - re[n - k])
            imags.append(None if k == 0 else (im[k] - im[n - k] if parity == 0 else im[k] + im[n - k]))
        for b in range(parity, n, 2):
            terms = []
            for k in range(n // 2):
                weight = scale if k == 0 else 2.0 * scale
                terms.append((weight * unit(math.cos, b, k, n), reals[k]))
                if k:
                    terms.append((-weight * unit(math.sin, b, k, n), imags[k]))
            if parity == 0:
                terms.append((2.0 * scale * unit(math.cos, b, n // 2, n), re[n // 2]))
            else:
                terms.append((-2.0 * scale * unit(math.sin, b, n // 2, n), im[n // 2]))
            terms = [(c if abs(c) > 1e-9 * scale else 0.0, v) for c, v in terms]
            store(b, weighted([(c / scale, v) for c, v in terms]) * scale)


ROWS = 16


def conv_kernel(n, x_ref, table, y_ref, spec, wide):
    channels = y_ref.shape[1]

    def front_step(i, _):
        rows = pl.ds(pl.multiple_of(i * ROWS, ROWS), ROWS)
        front(n, rows, lambda b: x_ref[b, rows, :].astype(f32), spec)
        return 0

    lax.fori_loop(0, 2 * channels // ROWS, front_step, 0)
    middle(0, channels, True, spec, table, wide)
    middle(n, channels, True, spec, table, wide)

    def middle_step(k1, _):
        middle(k1, channels, False, spec, table, wide)
        return 0

    lax.fori_loop(1, n, middle_step, 0)

    height = min(ROWS, channels)

    def back_step(i, _):
        rows = pl.ds(pl.multiple_of(i * height, height), height)

        def store(b, value):
            y_ref[b, rows, :] = value.astype(bf16)

        back(n, rows, wide, store)
        return 0

    lax.fori_loop(0, channels // height, back_step, 0)


def per_device(signal, pre_gate, post_gate, filter_taps, skip_gain, out_weight):
    channels_here, tokens_here = signal.shape
    n = lax.axis_size("ctx")
    mine = channels_here // n
    gated_input = signal.astype(f32) * pre_gate.astype(f32)
    stacked = jnp.stack([gated_input.astype(bf16), filter_taps.astype(bf16)])
    stacked = stacked.reshape(2, n, mine, tokens_here).transpose(1, 0, 2, 3).reshape(n, 2 * mine, tokens_here)
    blocks = lax.all_to_all(stacked, "ctx", split_axis=0, concat_axis=0, tiled=True)
    table = jnp.asarray(freq_tables(n, tokens_here))
    conv = pl.pallas_call(
        functools.partial(conv_kernel, n),
        out_shape=jax.ShapeDtypeStruct((n, mine, tokens_here), bf16),
        in_specs=[pl.BlockSpec(memory_space=pltpu.VMEM)] * 2,
        out_specs=pl.BlockSpec(memory_space=pltpu.VMEM),
        scratch_shapes=[
            pltpu.VMEM((n + 1, 2 * mine, 2 * tokens_here), bf16),
            pltpu.VMEM((n + 1, mine, 2 * tokens_here), f32),
        ],
        compiler_params=pltpu.CompilerParams(vmem_limit_bytes=48 * 1024 * 1024),
    )(blocks, table)
    conv = lax.all_to_all(conv, "ctx", split_axis=0, concat_axis=0, tiled=True)
    convolved = conv.reshape(channels_here, tokens_here).astype(f32)
    mixed = (post_gate.astype(f32) * (convolved + skip_gain[:, None] * gated_input)).astype(bf16)
    return lax.psum_scatter(
        lax.dot_general(
            out_weight, mixed, (((0,), (0,)), ((), ())), preferred_element_type=f32
        ).astype(bf16),
        "tp",
        scatter_dimension=0,
        tiled=True,
    )


def solution(mesh):
    return jax.shard_map(
        per_device,
        mesh=mesh,
        in_specs=(
            P("tp", "ctx"),
            P("tp", "ctx"),
            P("tp", "ctx"),
            P("tp", "ctx"),
            P("tp"),
            P("tp", None),
        ),
        out_specs=P("tp", "ctx"),
        check_vma=False,
    )
```

time: 341 us -> 113 us (0.33); the launches traced: 335 us -> 112 us
  waiting for transfers between devices: 136 us -> 30.7 us
  matrix products: 59.4 us -> 3.92 us
  blocking collectives: 84.8 us -> 50.3 us
  local copies, waits for them, and re-layouts: 29.7 us -> 2.06 us
  starting transfers between devices: 8.43 us -> 0.03 us
  Pallas kernels: 0 us -> 8.23 us
    all_to_all x2 -> x0, waiting for transfers between devices: 105 us -> none  [the longest x1 92 us: per_device(): lax.all_to_all(front_section(blocks, devices).astype(jnp.bfloat16), 'ctx'...]
    dot_general x12 -> x0, matrix products: 52.3 us -> none  [the longest x8 46.6 us: matmul_high(): return jnp.matmul(left, right, precision=highest)]
    all_to_all x2, blocking collectives: 84.8 us -> 50.3 us  [the longest x1 32.8 us: per_device(): lax.all_to_all(stacked, 'ctx', split_axis=0, concat_axis=0, tiled=True)]
    another operation x3 -> x0, local copies, waits for them, and re-layouts: 9.72 us -> none  [the longest x1 4.35 us: middle_section(): return jnp.stack([out_real, out_imag])]
    all_to_all x2 -> x0, starting transfers between devices: 8.39 us -> none  [the longest x1 4.76 us: per_device(): lax.all_to_all(front_section(blocks, devices).astype(jnp.bfloat16), 'ctx'...]
    pallas_call x0 -> x1, Pallas kernels: none -> 8.23 us  [per_device(): pl.pallas_call(functools.partial(conv_kernel, n), out_shape=jax.ShapeDtyp...]
    slice x6 -> x0, local copies, waits for them, and re-layouts: 6.84 us -> none  [the longest x2 3.49 us: back_section(): wide[1]]
    unnamed x14 -> x10, local copies, waits for them, and re-layouts: 5.57 us -> 0.02 us
  transfers between devices with their start and end apart: 3 -> 1, of which waited for: 3 -> 1; matrix products, arithmetic and copies ran while one was open for 0% -> 0% of each run, Pallas kernels for 0% -> 0%
where the time goes in v1:
time: 113 us; the launch traced here: 112 us
  blocking collectives  50.3 us (45%)
  waiting for transfers between devices  30.7 us (27%)
  between operations  13.4 us (12%)
  Pallas kernels  8.23 us (7%)
  matrix products  3.92 us (3%)
  other arithmetic  3.61 us (3%)
  local copies, waits for them, and re-layouts  2.06 us (2%)
    all_to_all x1, blocking collectives, per_device(): lax.all_to_all(stacked, 'ctx', split_axis=0, concat_axis=0, tiled=True)  32.8 us
    reduce_scatter x1, waiting for transfers between devices, per_device(): lax.psum_scatter(lax.dot_general(out_weight, mixed, (((0,), (0,)), ((), (...  30.7 us
    all_to_all x1, blocking collectives, per_device(): conv = lax.all_to_all(conv, 'ctx', split_axis=0, concat_axis=0, tiled=True)  17.5 us
    pallas_call x1, Pallas kernels, per_device(): pl.pallas_call(functools.partial(conv_kernel, n), out_shape=jax.ShapeDtyp...  8.23 us
    dot_general x1, matrix products, per_device(): lax.dot_general(out_weight, mixed, (((0,), (0,)), ((), ())), preferred_el...  3.92 us
    convert_element_type x2, other arithmetic, per_device(): stacked = jnp.stack([gated_input.astype(bf16), filter_taps.astype(bf16)])  3.51 us
  transfers between devices with their start and end apart: 1, of which 1 were waited for; matrix products, arithmetic and copies ran while one was open for 0% of the time, Pallas kernels for 0%

profile of v1, /device:TPU:0, one launch (start us, length us, event | category | flops | bytes accessed | tf_op | source)
XLA Modules:
  0.0 112.3 jit_solution(15415652167925759535)
XLA Ops:
  6.5 0.0 copy-start.1
  6.5 0.0 copy-start.2
  6.5 0.0 copy-start.4
  6.5 0.0 copy-start.3
  6.5 0.0 reduce-scatter.2.cloned.1.call-start
  6.6 0.0 copy-start
  6.6 1.4 %convert_element_type.34 = bf16[1024,256]{1,0:T(8,128)(2,1)S(1)} convert(f32[1024,256]{1,0:T(8,128)} %param.10) | non-fusion elementwise | flops 262144 | bytes 1572864 | tf_op jit(solution)/shard_map/convert_element_type | solution.py:141
  8.0 2.1 %fusion.3 = bf16[1024,256]{1,0:T(8,128)(2,1)S(1)} fusion(bf16[1024,256]{1,0:T(8,128)(2,1)} %param.8, bf16[1024,256]{1,0:T(8,128)(2,1)} %param.7), kind=kLoop, calls=%fused_computation.7 | loop fusion | flops 1048576 | bytes 1572864 | tf_op jit(solution)/shard_map/convert_element_type | solution.py:141
  10.1 0.1 pad_maximum_fusion
  10.2 32.8 %all_to_all.10.x_ref = bf16[8,256,256]{2,1,0:T(8,128)(2,1)S(1)} all-to-all(bf16[8,256,256]{2,1,0:T(8,128)(2,1)S(1)} %bitcast.14), channel_id=1, replica_groups=mesh['ctx'=8,'tp'=4] {'ctx'}, dimensions={0} | all-to-all | bytes 2097152 | tf_op jit(solution)/shard_map/all_to_all | solution.py:143
  43.0 8.2 %shard_map.73 = bf16[8,128,256]{2,1,0:T(8,128)(2,1)S(1)} custom-call(bf16[8,256,256]{2,1,0:T(8,128)(2,1)S(1)} %all_to_all.10.x_ref, bf16[9,512,512]{2,1,0:T(8,128)(2,1)} %constant.2.clone.table), custom_call_target="tpu_custom_call" | custom-call | tf_op jit(solution)/shard_map/pallas_call | solution.py:145
  51.3 17.5 %all_to_all.11 = bf16[8,128,256]{2,1,0:T(8,128)(2,1)S(1)} all-to-all(bf16[8,128,256]{2,1,0:T(8,128)(2,1)S(1)} %shard_map.73), channel_id=1, replica_groups=mesh['ctx'=8,'tp'=4] {'ctx'}, dimensions={0} | all-to-all | bytes 1048576 | tf_op jit(solution)/shard_map/all_to_all | solution.py:156
  68.8 0.0 copy-done.1
  68.8 0.0 copy-done.2
  68.8 0.0 copy-done.4
  68.8 0.0 copy-done.3
  68.8 0.0 copy-done
  68.8 3.9 %fusion = bf16[4096,256]{0,1:T(8,128)(2,1)} fusion(bf16[1024,4096]{1,0:T(8,128)(2,1)S(1)} %copy-done, bf16[1024,256]{1,0:T(8,128)(2,1)S(1)} %bitcast.15, bf16[1024,256]{1,0:T(8,128)(2,1)S(1)} %copy-done.3, bf16[1024,256]{1,0:T(8,128)(2,1)S(1)} %copy-done.1, bf16[1024,256]{1,0:T(8,128)(2,1)S(1)} %copy-done.2, f32[1024]{0:T(1024)S(1)} %copy-done.4), kind=kOutput, calls=%fused_computation.1 | convolution fusion | flops 2150891520 | bytes 12587008 | tf_op jit(solution)/shard_map/dot_general | solution.py:160
  72.8 0.0 reduce-scatter.2.cloned.1.call-update
  72.8 30.7 %reduce-scatter.2.cloned.1.call-done = bf16[1024,256]{0,1:T(8,128)(2,1)} async-done(((bf16[4096,256]{0,1:T(8,128)(2,1)}), bf16[1024,256]{0,1:T(8,128)(2,1)}) %reduce-scatter.2.cloned.1.call-update) | async-done | bytes 524304 | tf_op jit(solution)/shard_map/reduce_scatter | solution.py:159
  103.4 2.0 %copy.10 = bf16[1024,256]{1,0:T(8,128)(2,1)} copy(bf16[1024,256]{0,1:T(8,128)(2,1)} %reduce-scatter.2.cloned.1.call-done) | data formatting | bytes 1048576 | tf_op jit(solution)/shard_map/reduce_scatter | solution.py:159
Async XLA Ops:
  6.5 62.3 %copy-start.1 = (bf16[1024,256]{1,0:T(8,128)(2,1)S(1)}, bf16[1024,256]{1,0:T(8,128)(2,1)}, u32[]{:S(2)}) copy-start(bf16[1024,256]{1,0:T(8,128)(2,1)} %param.8) | copy-start | bytes 1572868
  6.5 62.3 %copy-start.2 = (bf16[1024,256]{1,0:T(8,128)(2,1)S(1)}, bf16[1024,256]{1,0:T(8,128)(2,1)}, u32[]{:S(2)}) copy-start(bf16[1024,256]{1,0:T(8,128)(2,1)} %param.7) | copy-start | bytes 1572868
  6.5 62.3 %copy-start.4 = (f32[1024]{0:T(1024)S(1)}, f32[1024]{0:T(1024)}, u32[]{:S(2)}) copy-start(f32[1024]{0:T(1024)} %param.11) | copy-start | bytes 12292
  6.5 62.3 %copy-start.3 = (bf16[1024,256]{1,0:T(8,128)(2,1)S(1)}, bf16[1024,256]{1,0:T(8,128)(2,1)}, u32[]{:S(2)}) copy-start(bf16[1024,256]{1,0:T(8,128)(2,1)} %param.9) | copy-start | bytes 1572868
  6.5 96.9 %reduce-scatter.2.cloned.1.call-start = ((), (), s32[]{:S(2)}) async-start(), calls=%async_computation.3 | async-start | bytes 2621440 | tf_op jit(solution)/shard_map/reduce_scatter | solution.py:159
  6.6 62.2 %copy-start = (bf16[1024,4096]{1,0:T(8,128)(2,1)S(1)}, bf16[1024,4096]{1,0:T(8,128)(2,1)}, u32[]{:S(2)}) copy-start(bf16[1024,4096]{1,0:T(8,128)(2,1)} %param.12) | copy-start | bytes 25165828
Sparse Core Ops, SparseCore 0:
  72.9 30.4 reduce-scatter.1

commit v2 on v1

--- a/solution.py
+++ b/solution.py
@@ -133,7 +133,7 @@
     lax.fori_loop(0, channels // height, back_step, 0)
 
 
-def per_device(signal, pre_gate, post_gate, filter_taps, skip_gain, out_weight):
+def per_device_generic(signal, pre_gate, post_gate, filter_taps, skip_gain, out_weight):
     channels_here, tokens_here = signal.shape
     n = lax.axis_size("ctx")
     mine = channels_here // n
@@ -166,6 +166,283 @@
     )
 
 
+MESH = pl.DeviceIdType.MESH
+HALVES = 2
+SUBS = 2
+
+
+def fused_kernel(
+    n, sig, pre, post, taps, skip, weight_hbm, table_hbm, out,
+    x_send, x_recv, spec, wide, y_send, y_recv, table, weight, mixed_t, part, a_send, a_recv, c_send, c_recv,
+    load_sem, xs_sem, xr_sem, ys_sem, yr_sem, as_sem, ar_sem, cs_sem, cr_sem,
+):
+    me = lax.axis_index("ctx")
+    tp = lax.axis_index("tp")
+    row, core = tp // 2, tp % 2
+    partner = row * 2 + (1 - core)
+    across = (1 - row) * 2 + core
+    channels, width = sig.shape
+    half = channels // HALVES
+    ch = half // n
+    feats = out.shape[0]
+    sub = feats // SUBS
+    order = sorted(range(1, n), key=lambda d: abs(d - n // 2))
+
+    loads = [pltpu.make_async_copy(table_hbm, table, load_sem.at[0])]
+    for f in range(4):
+        loads.append(
+            pltpu.make_async_copy(weight_hbm.at[:, pl.ds(f * feats, feats)], weight.at[f], load_sem.at[1 + f])
+        )
+    for load in loads:
+        load.start()
+
+    barrier = pltpu.get_barrier_semaphore()
+    for d in range(1, n):
+        pl.semaphore_signal(barrier, inc=1, device_id={"ctx": lax.rem(me + d, n)}, device_id_type=MESH)
+    pl.semaphore_signal(barrier, inc=1, device_id={"tp": partner}, device_id_type=MESH)
+    pl.semaphore_signal(barrier, inc=1, device_id={"tp": across}, device_id_type=MESH)
+
+    def owned(h, peer):
+        return pl.ds(pl.multiple_of(h * half + peer * ch, ch), ch)
+
+    def gated(rows):
+        return sig[rows, :].astype(f32) * pre[rows, :].astype(f32)
+
+    x_copies = {}
+    for h in range(HALVES):
+        for d in order:
+            rows = owned(h, lax.rem(me + d, n))
+            x_send[h, d, :ch, :] = gated(rows).astype(bf16)
+            x_send[h, d, ch:, :] = taps[rows, :].astype(bf16)
+        if h == 0:
+            pl.semaphore_wait(barrier, n + 1)
+        for d in order:
+            copy = pltpu.make_async_remote_copy(
+                src_ref=x_send.at[h, d],
+                dst_ref=x_recv.at[h, me],
+                send_sem=xs_sem.at[h, d],
+                recv_sem=xr_sem.at[h, d],
+                device_id={"ctx": lax.rem(me + d, n)},
+                device_id_type=MESH,
+            )
+            copy.start()
+            x_copies[h, d] = copy
+    for h in range(HALVES):
+        rows = owned(h, me)
+        x_recv[h, me, :ch, :] = gated(rows).astype(bf16)
+        x_recv[h, me, ch:, :] = taps[rows, :].astype(bf16)
+    loads[0].wait()
+
+    y_copies = {}
+
+    def mix(h):
+        for d in order:
+            y_copies[h, d].wait_recv()
+        y_recv[owned(h, me), :] = y_send[h, me]
+        step = 128
+        for j in range(half // step):
+            rows = pl.ds(h * half + j * step, step)
+            value = post[rows, :].astype(f32) * (y_recv[rows, :].astype(f32) + skip[rows, :] * gated(rows))
+            mixed_t[:, pl.ds(h * half + j * step, step)] = value.T.astype(bf16)
+
+    for h in range(HALVES):
+        for d in order:
+            x_copies[h, d].wait_recv()
+
+        def front_step(i, _):
+            rows = pl.ds(pl.multiple_of(i * ROWS, ROWS), ROWS)
+            front(n, rows, lambda b: x_recv[h, b, rows, :].astype(f32), spec)
+            return 0
+
+        lax.fori_loop(0, 2 * ch // ROWS, front_step, 0)
+        middle(0, ch, True, spec, table, wide)
+        middle(n, ch, True, spec, table, wide)
+
+        def middle_step(k1, _):
+            middle(k1, ch, False, spec, table, wide)
+            return 0
+
+        lax.fori_loop(1, n, middle_step, 0)
+
+        def back_step(i, _):
+            rows = pl.ds(pl.multiple_of(i * ROWS, ROWS), ROWS)
+
+            def store(b, value):
+                y_send[h, b, rows, :] = value.astype(bf16)
+
+            back(n, rows, wide, store)
+            return 0
+
+        lax.fori_loop(0, ch // ROWS, back_step, 0)
+        for d in order:
+            peer = lax.rem(me + d, n)
+            copy = pltpu.make_async_remote_copy(
+                src_ref=y_send.at[h, peer],
+                dst_ref=y_recv.at[owned(h, me)],
+                send_sem=ys_sem.at[h, d],
+                recv_sem=yr_sem.at[h, d],
+                device_id={"ctx": peer},
+                device_id_type=MESH,
+            )
+            copy.start()
+            y_copies[h, d] = copy
+
+    for load in loads[1:]:
+        load.wait()
+    tile = 256
+
+    def columns(t):
+        return pl.ds(pl.multiple_of(t * tile, tile), tile)
+
+    for h in range(HALVES - 1):
+        mix(h)
+        for f in range(4):
+
+            def partial_step(t, _):
+                term = jnp.dot(
+                    mixed_t[:, h * half : (h + 1) * half],
+                    weight[f, h * half : (h + 1) * half, columns(t)],
+                    preferred_element_type=f32,
+                )
+                part[f, :, columns(t)] = term if h == 0 else part[f, :, columns(t)] + term
+                return 0
+
+            lax.fori_loop(0, feats // tile, partial_step, 0)
+
+    last = HALVES - 1
+    mix(last)
+
+    def project(f, t):
+        return part[f, :, columns(t)] + jnp.dot(
+            mixed_t[:, last * half :], weight[f, last * half :, columns(t)], preferred_element_type=f32
+        )
+
+    per_sub = sub // tile
+    a_copies, c_copies = {}, {}
+
+    def send_partner(slot, s, f):
+        def step(t, _):
+            a_send[slot, s, :, columns(t)] = project(f, s * per_sub + t).astype(bf16)
+            return 0
+
+        lax.fori_loop(0, per_sub, step, 0)
+        copy = pltpu.make_async_remote_copy(
+            src_ref=a_send.at[slot, s],
+            dst_ref=a_recv.at[slot, s],
+            send_sem=as_sem.at[slot, s],
+            recv_sem=ar_sem.at[slot, s],
+            device_id={"tp": partner},
+            device_id_type=MESH,
+        )
+        copy.start()
+        a_copies[slot, s] = copy
+
+    for s in range(SUBS):
+        send_partner(0, s, (1 - row) * 2 + (1 - core))
+    for s in range(SUBS):
+        a_copies[0, s].wait_recv()
+
+        def across_step(t, _):
+            total = project(across, s * per_sub + t) + a_recv[0, s, :, columns(t)].astype(f32)
+            c_send[s, :, columns(t)] = total.astype(bf16)
+            return 0
+
+        lax.fori_loop(0, per_sub, across_step, 0)
+        copy = pltpu.make_async_remote_copy(
+            src_ref=c_send.at[s],
+            dst_ref=c_recv.at[s],
+            send_sem=cs_sem.at[s],
+            recv_sem=cr_sem.at[s],
+            device_id={"tp": across},
+            device_id_type=MESH,
+        )
+        copy.start()
+        c_copies[s] = copy
+    for s in range(SUBS):
+        send_partner(1, s, partner)
+    for s in range(SUBS):
+        a_copies[1, s].wait_recv()
+
+        def own_step(t, _):
+            where = columns(s * per_sub + t)
+            part[tp, :, where] = project(tp, s * per_sub + t) + a_recv[1, s, :, columns(t)].astype(f32)
+            return 0
+
+        lax.fori_loop(0, per_sub, own_step, 0)
+    for s in range(SUBS):
+        c_copies[s].wait_recv()
+
+        def out_step(t, _):
+            where = columns(s * per_sub + t)
+            total = part[tp, :, where] + c_recv[s, :, columns(t)].astype(f32)
+            out[where, :] = total.T.astype(bf16)
+            return 0
+
+        lax.fori_loop(0, per_sub, out_step, 0)
+    for group in (x_copies, y_copies, a_copies, c_copies):
+        for copy in group.values():
+            copy.wait_send()
+
+
+def per_device_fused(signal, pre_gate, post_gate, filter_taps, skip_gain, out_weight):
+    channels, width = signal.shape
+    n = lax.axis_size("ctx")
+    feats = out_weight.shape[1] // 4
+    half = channels // HALVES
+    ch = half // n
+    sub = feats // SUBS
+    vmem = pl.BlockSpec(memory_space=pltpu.VMEM)
+    hbm = pl.BlockSpec(memory_space=pl.ANY)
+    dma = pltpu.SemaphoreType.DMA
+    return pl.pallas_call(
+        functools.partial(fused_kernel, n),
+        out_shape=jax.ShapeDtypeStruct((feats, width), bf16),
+        in_specs=[vmem] * 5 + [hbm] * 2,
+        out_specs=vmem,
+        scratch_shapes=[
+            pltpu.VMEM((HALVES, n, 2 * ch, width), bf16),
+            pltpu.VMEM((HALVES, n, 2 * ch, width), bf16),
+            pltpu.VMEM((n + 1, 2 * ch, 2 * width), bf16),
+            pltpu.VMEM((n + 1, ch, 2 * width), f32),
+            pltpu.VMEM((HALVES, n, ch, width), bf16),
+            pltpu.VMEM((channels, width), bf16),
+            pltpu.VMEM((n + 1, 2 * width, 2 * width), bf16),
+            pltpu.VMEM((4, channels, feats), bf16),
+            pltpu.VMEM((width, channels), bf16),
+            pltpu.VMEM((4, width, feats), f32),
+            pltpu.VMEM((2, SUBS, width, sub), bf16),
+            pltpu.VMEM((2, SUBS, width, sub), bf16),
+            pltpu.VMEM((SUBS, width, sub), bf16),
+            pltpu.VMEM((SUBS, width, sub), bf16),
+            dma((5,)),
+            dma((HALVES, n)),
+            dma((HALVES, n)),
+            dma((HALVES, n)),
+            dma((HALVES, n)),
+            dma((2, SUBS)),
+            dma((2, SUBS)),
+            dma((SUBS,)),
+            dma((SUBS,)),
+        ],
+        compiler_params=pltpu.CompilerParams(
+            collective_id=0, has_side_effects=True, vmem_limit_bytes=56 * 1024 * 1024
+        ),
+    )(
+        signal, pre_gate, post_gate, filter_taps, skip_gain[:, None], out_weight,
+        jnp.asarray(freq_tables(n, width)),
+    )
+
+
+def per_device(signal, *rest):
+    channels, width = signal.shape
+    features = rest[-1].shape[1]
+    n, tp = lax.axis_size("ctx"), lax.axis_size("tp")
+    fits = n <= 8 and n % 2 == 0 and tp == 4 and width % 256 == 0
+    fits = fits and channels % (HALVES * n * 16) == 0 and channels % (HALVES * 128) == 0
+    fits = fits and features % (4 * SUBS * 256) == 0
+    return (per_device_fused if fits else per_device_generic)(signal, *rest)
+
+
 def solution(mesh):
     return jax.shard_map(
         per_device,

time: 113 us -> 66.2 us (0.59)
  Pallas kernels: 8.23 us -> 62.4 us
  blocking collectives: 50.3 us -> 0 us
  waiting for transfers between devices: 30.7 us -> 0 us
  between operations: 13.4 us -> 0.01 us
  matrix products: 3.92 us -> 0 us
  other arithmetic: 3.61 us -> 0 us
  local copies, waits for them, and re-layouts: 2.06 us -> 3.57 us
    pallas_call x1, Pallas kernels: 8.23 us -> 62.4 us  [per_device_fused(): pl.pallas_call(functools.partial(fused_kernel, n), out_shape=jax.ShapeDty...]
    all_to_all x2 -> x0, blocking collectives: 50.3 us -> none  [the longest x1 32.8 us: per_device(): lax.all_to_all(stacked, 'ctx', split_axis=0, concat_axis=0, tiled=True)]
    reduce_scatter x1 -> x0, waiting for transfers between devices: 30.7 us -> none  [per_device(): lax.psum_scatter(lax.dot_general(out_weight, mixed, (((0,), (0,)), ((), (...]
    dot_general x1 -> x0, matrix products: 3.92 us -> none  [per_device(): lax.dot_general(out_weight, mixed, (((0,), (0,)), ((), ())), preferred_el...]
    convert_element_type x2 -> x0, other arithmetic: 3.51 us -> none  [per_device(): stacked = jnp.stack([gated_input.astype(bf16), filter_taps.astype(bf16)])]
    reduce_scatter x1 -> x0, local copies, waits for them, and re-layouts: 2.04 us -> none  [per_device(): lax.psum_scatter(lax.dot_general(out_weight, mixed, (((0,), (0,)), ((), (...]
    unnamed x10 -> x1, local copies, waits for them, and re-layouts: 0.02 us -> 1.87 us
    broadcast_in_dim x0 -> x1, local copies, waits for them, and re-layouts: none -> 1.71 us  [per_device_fused(): skip_gain[:, None]]
  transfers between devices with their start and end apart: 1 -> 0, of which waited for: 1 -> 0; matrix products, arithmetic and copies ran while one was open for 0% -> 0% of each run, Pallas kernels for 0% -> 0%
where the time goes in v2:
time: 66.2 us; the launch traced here: 65.9 us
  Pallas kernels  62.4 us (94%)
  local copies, waits for them, and re-layouts  3.57 us (5%)
    pallas_call x1, Pallas kernels, per_device_fused(): pl.pallas_call(functools.partial(fused_kernel, n), out_shape=jax.ShapeDty...  62.4 us
    unnamed x1, local copies, waits for them, and re-layouts  1.87 us
    broadcast_in_dim x1, local copies, waits for them, and re-layouts, per_device_fused(): skip_gain[:, None]  1.71 us

profile of v2, /device:TPU:0, one launch (start us, length us, event | category | flops | bytes accessed | tf_op | source)
XLA Modules:
  0.0 65.9 jit_solution(11340484640187582659)
XLA Ops:
  0.0 1.7 %copy.8.skip = f32[1024,1]{1,0:T(8,128)} copy(f32[1024,1]{0,1:T(1,128)} %bitcast.1) | data formatting | bytes 8192 | tf_op jit(solution)/shard_map/broadcast_in_dim | solution.py:431
  1.7 62.4 %shard_map.73 = bf16[1024,256]{1,0:T(8,128)(2,1)} custom-call(bf16[1024,256]{1,0:T(8,128)(2,1)} %sig.1, bf16[1024,256]{1,0:T(8,128)(2,1)} %pre.1, bf16[1024,256]{1,0:T(8,128)(2,1)} %post.1, f32[1024,256]{1,0:T(8,128)} %taps.1, f32[1024,1]{1,0:T(8,128)} %copy.8.skip, bf16[1024,4096]{1,0:T(8,128)(2,1)} %weight_hbm.1, bf16[9,512,512]{2,1,0:T(8,128)(2,1)} %constant.2.clone.table_hbm), custom_call_target="tpu_custom_call" | custom-call | tf_op jit(solution)/shard_map/pallas_call | solution.py:397
  64.1 1.9 %copy.10 = bf16[1024,256]{1,0:T(8,128)(2,1)} copy(bf16[1024,256]{1,0:T(8,128)(2,1)} %shard_map.73) | data formatting | bytes 1048576

commit v3 on v2

--- a/solution.py
+++ b/solution.py
@@ -185,8 +185,17 @@
     half = channels // HALVES
     ch = half // n
     feats = out.shape[0]
-    sub = feats // SUBS
-    order = sorted(range(1, n), key=lambda d: abs(d - n // 2))
+    order = sorted(range(1, n), key=lambda m: -(m // 2))
+    span = width // SUBS
+
+    def peer_of(mask):
+        peer, bit = me, 1
+        while bit < n:
+            if mask // bit % 2:
+                peer = peer + bit * (1 - 2 * ((me // bit) % 2))
+            bit *= 2
+        return peer
+
 
     loads = [pltpu.make_async_copy(table_hbm, table, load_sem.at[0])]
     for f in range(4):
@@ -198,7 +207,7 @@
 
     barrier = pltpu.get_barrier_semaphore()
     for d in range(1, n):
-        pl.semaphore_signal(barrier, inc=1, device_id={"ctx": lax.rem(me + d, n)}, device_id_type=MESH)
+        pl.semaphore_signal(barrier, inc=1, device_id={"ctx": peer_of(d)}, device_id_type=MESH)
     pl.semaphore_signal(barrier, inc=1, device_id={"tp": partner}, device_id_type=MESH)
     pl.semaphore_signal(barrier, inc=1, device_id={"tp": across}, device_id_type=MESH)
 
@@ -211,7 +220,7 @@
     x_copies = {}
     for h in range(HALVES):
         for d in order:
-            rows = owned(h, lax.rem(me + d, n))
+            rows = owned(h, peer_of(d))
             x_send[h, d, :ch, :] = gated(rows).astype(bf16)
             x_send[h, d, ch:, :] = taps[rows, :].astype(bf16)
         if h == 0:
@@ -222,7 +231,7 @@
                 dst_ref=x_recv.at[h, me],
                 send_sem=xs_sem.at[h, d],
                 recv_sem=xr_sem.at[h, d],
-                device_id={"ctx": lax.rem(me + d, n)},
+                device_id={"ctx": peer_of(d)},
                 device_id_type=MESH,
             )
             copy.start()
@@ -234,58 +243,71 @@
     loads[0].wait()
 
     y_copies = {}
-
-    def mix(h):
+    skip_t = skip[...].T
+
+    def mix(h, t):
         for d in order:
-            y_copies[h, d].wait_recv()
-        y_recv[owned(h, me), :] = y_send[h, me]
+            y_copies[h, t, d].wait_recv()
+        y_recv[t, owned(h, me), :] = y_send[h, t, me]
         step = 128
-        for j in range(half // step):
-            rows = pl.ds(h * half + j * step, step)
-            value = post[rows, :].astype(f32) * (y_recv[rows, :].astype(f32) + skip[rows, :] * gated(rows))
-            mixed_t[:, pl.ds(h * half + j * step, step)] = value.T.astype(bf16)
-
-    for h in range(HALVES):
+        tokens = pl.ds(t * span, span)
+        for j in range(h * half // step, (h + 1) * half // step):
+            rows = pl.ds(j * step, step)
+            gate_in = sig[rows, tokens].astype(f32) * pre[rows, tokens].astype(f32)
+            conv = y_recv[t, rows, :].astype(f32)
+            value = post[rows, tokens].astype(f32) * (conv + skip_t[:, j : j + 1] * gate_in)
+            mixed_t[tokens, rows] = value.T.astype(bf16)
+
+    def send_back(h, t):
         for d in order:
-            x_copies[h, d].wait_recv()
-
-        def front_step(i, _):
-            rows = pl.ds(pl.multiple_of(i * ROWS, ROWS), ROWS)
-            front(n, rows, lambda b: x_recv[h, b, rows, :].astype(f32), spec)
-            return 0
-
-        lax.fori_loop(0, 2 * ch // ROWS, front_step, 0)
-        middle(0, ch, True, spec, table, wide)
-        middle(n, ch, True, spec, table, wide)
-
-        def middle_step(k1, _):
-            middle(k1, ch, False, spec, table, wide)
-            return 0
-
-        lax.fori_loop(1, n, middle_step, 0)
-
-        def back_step(i, _):
-            rows = pl.ds(pl.multiple_of(i * ROWS, ROWS), ROWS)
-
-            def store(b, value):
-                y_send[h, b, rows, :] = value.astype(bf16)
-
-            back(n, rows, wide, store)
-            return 0
-
-        lax.fori_loop(0, ch // ROWS, back_step, 0)
-        for d in order:
-            peer = lax.rem(me + d, n)
+            peer = peer_of(d)
             copy = pltpu.make_async_remote_copy(
-                src_ref=y_send.at[h, peer],
-                dst_ref=y_recv.at[owned(h, me)],
-                send_sem=ys_sem.at[h, d],
-                recv_sem=yr_sem.at[h, d],
+                src_ref=y_send.at[h, t, peer],
+                dst_ref=y_recv.at[t, owned(h, me)],
+                send_sem=ys_sem.at[h, t, d],
+                recv_sem=yr_sem.at[h, t, d],
                 device_id={"ctx": peer},
                 device_id_type=MESH,
             )
             copy.start()
-            y_copies[h, d] = copy
+            y_copies[h, t, d] = copy
+
+    for h in range(HALVES):
+        for d in order:
+            x_copies[h, d].wait_recv()
+        if h == HALVES - 1:
+            for earlier in range(h):
+                for t in range(SUBS):
+                    send_back(earlier, t)
+
+        def front_step(i, _):
+            rows = pl.ds(pl.multiple_of(i * ROWS, ROWS), ROWS)
+            front(n, rows, lambda b: x_recv[h, b, rows, :].astype(f32), spec)
+            return 0
+
+        lax.fori_loop(0, 2 * ch // ROWS, front_step, 0)
+        middle(0, ch, True, spec, table, wide)
+        middle(n, ch, True, spec, table, wide)
+
+        def middle_step(k1, _):
+            middle(k1, ch, False, spec, table, wide)
+            return 0
+
+        lax.fori_loop(1, n, middle_step, 0)
+
+        def back_step(i, _):
+            rows = pl.ds(pl.multiple_of(i * ROWS, ROWS), ROWS)
+
+            def store(b, value):
+                for t in range(SUBS):
+                    y_send[h, t, b, rows, :] = value[:, t * span : (t + 1) * span].astype(bf16)
+
+            back(n, rows, wide, store)
+            return 0
+
+        lax.fori_loop(0, ch // ROWS, back_step, 0)
+    for t in range(SUBS):
+        send_back(HALVES - 1, t)
 
     for load in loads[1:]:
         load.wait()
@@ -295,90 +317,98 @@
         return pl.ds(pl.multiple_of(t * tile, tile), tile)
 
     for h in range(HALVES - 1):
-        mix(h)
+        for t in range(SUBS):
+            mix(h, t)
         for f in range(4):
 
-            def partial_step(t, _):
+            def partial_step(c, _):
                 term = jnp.dot(
                     mixed_t[:, h * half : (h + 1) * half],
-                    weight[f, h * half : (h + 1) * half, columns(t)],
+                    weight[f, h * half : (h + 1) * half, columns(c)],
                     preferred_element_type=f32,
                 )
-                part[f, :, columns(t)] = term if h == 0 else part[f, :, columns(t)] + term
+                part[f, :, columns(c)] = term if h == 0 else part[f, :, columns(c)] + term
                 return 0
 
             lax.fori_loop(0, feats // tile, partial_step, 0)
 
     last = HALVES - 1
-    mix(last)
-
-    def project(f, t):
-        return part[f, :, columns(t)] + jnp.dot(
-            mixed_t[:, last * half :], weight[f, last * half :, columns(t)], preferred_element_type=f32
+    tiles = feats // tile
+
+    def project(f, t, c):
+        tokens = pl.ds(t * span, span)
+        return part[f, tokens, columns(c)] + jnp.dot(
+            mixed_t[tokens, last * half :], weight[f, last * half :, columns(c)], preferred_element_type=f32
         )
 
-    per_sub = sub // tile
     a_copies, c_copies = {}, {}
 
-    def send_partner(slot, s, f):
-        def step(t, _):
-            a_send[slot, s, :, columns(t)] = project(f, s * per_sub + t).astype(bf16)
-            return 0
-
-        lax.fori_loop(0, per_sub, step, 0)
+    def send_partner(slot, t, f):
+        def step(c, _):
+            a_send[slot, t, :, columns(c)] = project(f, t, c).astype(bf16)
+            return 0
+
+        lax.fori_loop(0, tiles, step, 0)
         copy = pltpu.make_async_remote_copy(
-            src_ref=a_send.at[slot, s],
-            dst_ref=a_recv.at[slot, s],
-            send_sem=as_sem.at[slot, s],
-            recv_sem=ar_sem.at[slot, s],
+            src_ref=a_send.at[slot, t],
+            dst_ref=a_recv.at[slot, t],
+            send_sem=as_sem.at[slot, t],
+            recv_sem=ar_sem.at[slot, t],
             device_id={"tp": partner},
             device_id_type=MESH,
         )
         copy.start()
-        a_copies[slot, s] = copy
-
-    for s in range(SUBS):
-        send_partner(0, s, (1 - row) * 2 + (1 - core))
-    for s in range(SUBS):
-        a_copies[0, s].wait_recv()
-
-        def across_step(t, _):
-            total = project(across, s * per_sub + t) + a_recv[0, s, :, columns(t)].astype(f32)
-            c_send[s, :, columns(t)] = total.astype(bf16)
-            return 0
-
-        lax.fori_loop(0, per_sub, across_step, 0)
+        a_copies[slot, t] = copy
+
+    for t in range(SUBS):
+        tokens = pl.ds(t * span, span)
+        mix(last, t)
+        send_partner(0, t, (1 - row) * 2 + (1 - core))
+
+        def ahead_step(c, _):
+            part[across, tokens, columns(c)] = project(across, t, c)
+            return 0
+
+        lax.fori_loop(0, tiles, ahead_step, 0)
+        a_copies[0, t].wait_recv()
+
+        def across_step(c, _):
+            total = part[across, tokens, columns(c)] + a_recv[0, t, :, columns(c)].astype(f32)
+            c_send[t, :, columns(c)] = total.astype(bf16)
+            return 0
+
+        lax.fori_loop(0, tiles, across_step, 0)
         copy = pltpu.make_async_remote_copy(
-            src_ref=c_send.at[s],
-            dst_ref=c_recv.at[s],
-            send_sem=cs_sem.at[s],
-            recv_sem=cr_sem.at[s],
+            src_ref=c_send.at[t],
+            dst_ref=c_recv.at[t],
+            send_sem=cs_sem.at[t],
+            recv_sem=cr_sem.at[t],
             device_id={"tp": across},
             device_id_type=MESH,
         )
         copy.start()
-        c_copies[s] = copy
-    for s in range(SUBS):
-        send_partner(1, s, partner)
-    for s in range(SUBS):
-        a_copies[1, s].wait_recv()
-
-        def own_step(t, _):
-            where = columns(s * per_sub + t)
-            part[tp, :, where] = project(tp, s * per_sub + t) + a_recv[1, s, :, columns(t)].astype(f32)
-            return 0
-
-        lax.fori_loop(0, per_sub, own_step, 0)
-    for s in range(SUBS):
-        c_copies[s].wait_recv()
-
-        def out_step(t, _):
-            where = columns(s * per_sub + t)
-            total = part[tp, :, where] + c_recv[s, :, columns(t)].astype(f32)
-            out[where, :] = total.T.astype(bf16)
-            return 0
-
-        lax.fori_loop(0, per_sub, out_step, 0)
+        c_copies[t] = copy
+    for t in range(SUBS):
+        send_partner(1, t, partner)
+    for t in range(SUBS):
+        tokens = pl.ds(t * span, span)
+        a_copies[1, t].wait_recv()
+
+        def own_step(c, _):
+            part[tp, tokens, columns(c)] = project(tp, t, c) + a_recv[1, t, :, columns(c)].astype(f32)
+            return 0
+
+        lax.fori_loop(0, tiles, own_step, 0)
+    for t in range(SUBS):
+        tokens = pl.ds(t * span, span)
+        c_copies[t].wait_recv()
+
+        def out_step(c, _):
+            total = part[tp, tokens, columns(c)] + c_recv[t, :, columns(c)].astype(f32)
+            out[columns(c), tokens] = total.T.astype(bf16)
+            return 0
+
+        lax.fori_loop(0, tiles, out_step, 0)
     for group in (x_copies, y_copies, a_copies, c_copies):
         for copy in group.values():
             copy.wait_send()
@@ -390,7 +420,7 @@
     feats = out_weight.shape[1] // 4
     half = channels // HALVES
     ch = half // n
-    sub = feats // SUBS
+    span = width // SUBS
     vmem = pl.BlockSpec(memory_space=pltpu.VMEM)
     hbm = pl.BlockSpec(memory_space=pl.ANY)
     dma = pltpu.SemaphoreType.DMA
@@ -404,21 +434,21 @@
             pltpu.VMEM((HALVES, n, 2 * ch, width), bf16),
             pltpu.VMEM((n + 1, 2 * ch, 2 * width), bf16),
             pltpu.VMEM((n + 1, ch, 2 * width), f32),
-            pltpu.VMEM((HALVES, n, ch, width), bf16),
-            pltpu.VMEM((channels, width), bf16),
+            pltpu.VMEM((HALVES, SUBS, n, ch, span), bf16),
+            pltpu.VMEM((SUBS, channels, span), bf16),
             pltpu.VMEM((n + 1, 2 * width, 2 * width), bf16),
             pltpu.VMEM((4, channels, feats), bf16),
             pltpu.VMEM((width, channels), bf16),
             pltpu.VMEM((4, width, feats), f32),
-            pltpu.VMEM((2, SUBS, width, sub), bf16),
-            pltpu.VMEM((2, SUBS, width, sub), bf16),
-            pltpu.VMEM((SUBS, width, sub), bf16),
-            pltpu.VMEM((SUBS, width, sub), bf16),
+            pltpu.VMEM((2, SUBS, span, feats), bf16),
+            pltpu.VMEM((2, SUBS, span, feats), bf16),
+            pltpu.VMEM((SUBS, span, feats), bf16),
+            pltpu.VMEM((SUBS, span, feats), bf16),
             dma((5,)),
             dma((HALVES, n)),
             dma((HALVES, n)),
-            dma((HALVES, n)),
-            dma((HALVES, n)),
+            dma((HALVES, SUBS, n)),
+            dma((HALVES, SUBS, n)),
             dma((2, SUBS)),
             dma((2, SUBS)),
             dma((SUBS,)),
@@ -428,7 +458,7 @@
             collective_id=0, has_side_effects=True, vmem_limit_bytes=56 * 1024 * 1024
         ),
     )(
-        signal, pre_gate, post_gate, filter_taps, skip_gain[:, None], out_weight,
+        signal, pre_gate, post_gate, filter_taps, skip_gain.reshape(channels // 128, 128), out_weight,
         jnp.asarray(freq_tables(n, width)),
     )
 
@@ -437,9 +467,9 @@
     channels, width = signal.shape
     features = rest[-1].shape[1]
     n, tp = lax.axis_size("ctx"), lax.axis_size("tp")
-    fits = n <= 8 and n % 2 == 0 and tp == 4 and width % 256 == 0
+    fits = n in (2, 4, 8) and tp == 4 and width % 256 == 0
     fits = fits and channels % (HALVES * n * 16) == 0 and channels % (HALVES * 128) == 0
-    fits = fits and features % (4 * SUBS * 256) == 0
+    fits = fits and features % (4 * 256) == 0
     return (per_device_fused if fits else per_device_generic)(signal, *rest)
 
 

time: 66.2 us -> 62.9 us (0.950)
  local copies, waits for them, and re-layouts: 3.57 us -> 1.87 us
  Pallas kernels: 62.4 us -> 60.8 us
    broadcast_in_dim x1 -> x0, local copies, waits for them, and re-layouts: 1.71 us -> none  [per_device_fused(): skip_gain[:, None]]
    pallas_call x1, Pallas kernels: 62.4 us -> 60.8 us  [per_device_fused(): pl.pallas_call(functools.partial(fused_kernel, n), out_shape=jax.ShapeDty...]
where the time goes in v3:
time: 62.9 us; the launch traced here: 62.7 us
  Pallas kernels  60.8 us (97%)
  local copies, waits for them, and re-layouts  1.87 us (3%)
    pallas_call x1, Pallas kernels, per_device_fused(): pl.pallas_call(functools.partial(fused_kernel, n), out_shape=jax.ShapeDty...  60.8 us
    unnamed x1, local copies, waits for them, and re-layouts  1.87 us

profile of v3, /device:TPU:0, one launch (start us, length us, event | category | flops | bytes accessed | tf_op | source)
XLA Modules:
  0.0 62.7 jit_solution(17365434283916588040)
XLA Ops:
  0.0 60.8 %shard_map.73 = bf16[1024,256]{1,0:T(8,128)(2,1)} custom-call(bf16[1024,256]{1,0:T(8,128)(2,1)} %sig.1, bf16[1024,256]{1,0:T(8,128)(2,1)} %pre.1, bf16[1024,256]{1,0:T(8,128)(2,1)} %post.1, f32[1024,256]{1,0:T(8,128)} %taps.1, f32[8,128]{1,0:T(8,128)} %bitcast.1, bf16[1024,4096]{1,0:T(8,128)(2,1)} %weight_hbm.1, bf16[9,512,512]{2,1,0:T(8,128)(2,1)} %constant.2.clone.table_hbm), custom_call_target="tpu_custom_call" | custom-call | tf_op jit(solution)/shard_map/pallas_call | solution.py:427
  60.8 1.9 %copy.9 = bf16[1024,256]{1,0:T(8,128)(2,1)} copy(bf16[1024,256]{1,0:T(8,128)(2,1)} %shard_map.73) | data formatting | bytes 1048576

commit v4 on v3

--- a/solution.py
+++ b/solution.py
@@ -63,11 +63,11 @@
 def middle(k1, channels, real_only, spec, table, wide):
     width = table.shape[-1] // 2
     depth = width if real_only else 2 * width
-    full = jnp.dot(spec[k1, :, :depth], table[k1, :depth, :], preferred_element_type=f32)
+    full = jnp.dot(spec[k1, : 2 * channels, :depth], table[k1, :depth, :], preferred_element_type=f32)
     ur, ui = full[:channels, :width], full[:channels, width:]
     hr, hi = full[channels:, :width], full[channels:, width:]
     prod = jnp.concatenate([ur * hr - ui * hi, ur * hi + ui * hr], axis=1).astype(bf16)
-    wide[k1, :, :depth] = lax.dot_general(
+    wide[k1, :channels, :depth] = lax.dot_general(
         prod, table[k1, :depth, :], (((1,), (1,)), ((), ())), preferred_element_type=f32
     )
 
@@ -167,8 +167,12 @@
 
 
 MESH = pl.DeviceIdType.MESH
-HALVES = 2
+CHUNKS = 2
 SUBS = 2
+
+
+def chunk_sizes(mine):
+    return (mine - mine // 4, mine // 4)
 
 
 def fused_kernel(
@@ -182,8 +186,8 @@
     partner = row * 2 + (1 - core)
     across = (1 - row) * 2 + core
     channels, width = sig.shape
-    half = channels // HALVES
-    ch = half // n
+    sizes = chunk_sizes(channels // n)
+    offsets = (0, sizes[0])
     feats = out.shape[0]
     order = sorted(range(1, n), key=lambda m: -(m // 2))
     span = width // SUBS
@@ -212,23 +216,30 @@
     pl.semaphore_signal(barrier, inc=1, device_id={"tp": across}, device_id_type=MESH)
 
     def owned(h, peer):
-        return pl.ds(pl.multiple_of(h * half + peer * ch, ch), ch)
+        return pl.ds(pl.multiple_of(n * offsets[h] + peer * sizes[h], 16), sizes[h])
+
+    def pair(h):
+        return pl.ds(2 * offsets[h], 2 * sizes[h])
 
     def gated(rows):
         return sig[rows, :].astype(f32) * pre[rows, :].astype(f32)
 
+    def fill(ref, slot, h, peer):
+        rows = owned(h, peer)
+        middle_row = 2 * offsets[h] + sizes[h]
+        ref[slot, pl.ds(2 * offsets[h], sizes[h]), :] = gated(rows).astype(bf16)
+        ref[slot, pl.ds(middle_row, sizes[h]), :] = taps[rows, :].astype(bf16)
+
     x_copies = {}
-    for h in range(HALVES):
+    for h in range(CHUNKS):
         for d in order:
-            rows = owned(h, peer_of(d))
-            x_send[h, d, :ch, :] = gated(rows).astype(bf16)
-            x_send[h, d, ch:, :] = taps[rows, :].astype(bf16)
+            fill(x_send, d, h, peer_of(d))
         if h == 0:
             pl.semaphore_wait(barrier, n + 1)
         for d in order:
             copy = pltpu.make_async_remote_copy(
-                src_ref=x_send.at[h, d],
-                dst_ref=x_recv.at[h, me],
+                src_ref=x_send.at[d, pair(h)],
+                dst_ref=x_recv.at[me, pair(h)],
                 send_sem=xs_sem.at[h, d],
                 recv_sem=xr_sem.at[h, d],
                 device_id={"ctx": peer_of(d)},
@@ -236,10 +247,8 @@
             )
             copy.start()
             x_copies[h, d] = copy
-    for h in range(HALVES):
-        rows = owned(h, me)
-        x_recv[h, me, :ch, :] = gated(rows).astype(bf16)
-        x_recv[h, me, ch:, :] = taps[rows, :].astype(bf16)
+    for h in range(CHUNKS):
+        fill(x_recv, me, h, me)
     loads[0].wait()
 
     y_copies = {}
@@ -248,10 +257,11 @@
     def mix(h, t):
         for d in order:
             y_copies[h, t, d].wait_recv()
-        y_recv[t, owned(h, me), :] = y_send[h, t, me]
+        y_recv[t, owned(h, me), :] = y_send[t, me, pl.ds(offsets[h], sizes[h])]
         step = 128
         tokens = pl.ds(t * span, span)
-        for j in range(h * half // step, (h + 1) * half // step):
+        first = n * offsets[h] // step
+        for j in range(first, first + n * sizes[h] // step):
             rows = pl.ds(j * step, step)
             gate_in = sig[rows, tokens].astype(f32) * pre[rows, tokens].astype(f32)
             conv = y_recv[t, rows, :].astype(f32)
@@ -262,7 +272,7 @@
         for d in order:
             peer = peer_of(d)
             copy = pltpu.make_async_remote_copy(
-                src_ref=y_send.at[h, t, peer],
+                src_ref=y_send.at[t, peer, pl.ds(offsets[h], sizes[h])],
                 dst_ref=y_recv.at[t, owned(h, me)],
                 send_sem=ys_sem.at[h, t, d],
                 recv_sem=yr_sem.at[h, t, d],
@@ -272,83 +282,68 @@
             copy.start()
             y_copies[h, t, d] = copy
 
-    for h in range(HALVES):
+    for h in range(CHUNKS):
         for d in order:
             x_copies[h, d].wait_recv()
-        if h == HALVES - 1:
-            for earlier in range(h):
-                for t in range(SUBS):
-                    send_back(earlier, t)
+        if h == 1:
+            send_back(0, 0)
+        size = sizes[h]
 
         def front_step(i, _):
             rows = pl.ds(pl.multiple_of(i * ROWS, ROWS), ROWS)
-            front(n, rows, lambda b: x_recv[h, b, rows, :].astype(f32), spec)
+            source = pl.ds(pl.multiple_of(2 * offsets[h] + i * ROWS, ROWS), ROWS)
+            front(n, rows, lambda b: x_recv[b, source, :].astype(f32), spec)
             return 0
 
-        lax.fori_loop(0, 2 * ch // ROWS, front_step, 0)
-        middle(0, ch, True, spec, table, wide)
-        middle(n, ch, True, spec, table, wide)
+        lax.fori_loop(0, 2 * size // ROWS, front_step, 0)
+        middle(0, size, True, spec, table, wide)
+        middle(n, size, True, spec, table, wide)
 
         def middle_step(k1, _):
-            middle(k1, ch, False, spec, table, wide)
+            middle(k1, size, False, spec, table, wide)
             return 0
 
         lax.fori_loop(1, n, middle_step, 0)
 
         def back_step(i, _):
             rows = pl.ds(pl.multiple_of(i * ROWS, ROWS), ROWS)
+            target = pl.ds(pl.multiple_of(offsets[h] + i * ROWS, ROWS), ROWS)
 
             def store(b, value):
                 for t in range(SUBS):
-                    y_send[h, t, b, rows, :] = value[:, t * span : (t + 1) * span].astype(bf16)
+                    y_send[t, b, target, :] = value[:, t * span : (t + 1) * span].astype(bf16)
 
             back(n, rows, wide, store)
             return 0
 
-        lax.fori_loop(0, ch // ROWS, back_step, 0)
-    for t in range(SUBS):
-        send_back(HALVES - 1, t)
+        lax.fori_loop(0, size // ROWS, back_step, 0)
+    send_back(1, 0)
+    for t in range(1, SUBS):
+        send_back(0, t)
+        send_back(1, t)
 
     for load in loads[1:]:
         load.wait()
     tile = 256
-
-    def columns(t):
-        return pl.ds(pl.multiple_of(t * tile, tile), tile)
-
-    for h in range(HALVES - 1):
-        for t in range(SUBS):
-            mix(h, t)
-        for f in range(4):
-
-            def partial_step(c, _):
-                term = jnp.dot(
-                    mixed_t[:, h * half : (h + 1) * half],
-                    weight[f, h * half : (h + 1) * half, columns(c)],
-                    preferred_element_type=f32,
-                )
-                part[f, :, columns(c)] = term if h == 0 else part[f, :, columns(c)] + term
-                return 0
-
-            lax.fori_loop(0, feats // tile, partial_step, 0)
-
-    last = HALVES - 1
     tiles = feats // tile
-
-    def project(f, t, c):
-        tokens = pl.ds(t * span, span)
-        return part[f, tokens, columns(c)] + jnp.dot(
-            mixed_t[tokens, last * half :], weight[f, last * half :, columns(c)], preferred_element_type=f32
+    head = n * sizes[0]
+
+    def columns(c):
+        return pl.ds(pl.multiple_of(c * tile, tile), tile)
+
+    def project(f, t, c, lo, hi):
+        return jnp.dot(
+            mixed_t[t * span : (t + 1) * span, lo:hi], weight[f, lo:hi, columns(c)], preferred_element_type=f32
         )
 
-    a_copies, c_copies = {}, {}
-
-    def send_partner(slot, t, f):
+    def each_tile(body):
         def step(c, _):
-            a_send[slot, t, :, columns(c)] = project(f, t, c).astype(bf16)
+            body(c)
             return 0
 
         lax.fori_loop(0, tiles, step, 0)
+
+    def to_partner(slot, t):
         copy = pltpu.make_async_remote_copy(
             src_ref=a_send.at[slot, t],
             dst_ref=a_recv.at[slot, t],
@@ -358,26 +353,39 @@
             device_id_type=MESH,
         )
         copy.start()
-        a_copies[slot, t] = copy
-
+        return copy
+
+    a_copies, c_copies = {}, {}
+    far = (1 - row) * 2 + (1 - core)
     for t in range(SUBS):
         tokens = pl.ds(t * span, span)
-        mix(last, t)
-        send_partner(0, t, (1 - row) * 2 + (1 - core))
-
-        def ahead_step(c, _):
-            part[across, tokens, columns(c)] = project(across, t, c)
-            return 0
-
-        lax.fori_loop(0, tiles, ahead_step, 0)
+        mix(0, t)
+
+        def early(c):
+            part[far, tokens, columns(c)] = project(far, t, c, 0, head)
+            part[across, tokens, columns(c)] = project(across, t, c, 0, head)
+
+        each_tile(early)
+        mix(1, t)
+
+        def far_rest(c):
+            total = part[far, tokens, columns(c)] + project(far, t, c, head, channels)
+            a_send[0, t, :, columns(c)] = total.astype(bf16)
+
+        each_tile(far_rest)
+        a_copies[0, t] = to_partner(0, t)
+
+        def across_rest(c):
+            part[across, tokens, columns(c)] += project(across, t, c, head, channels)
+
+        each_tile(across_rest)
         a_copies[0, t].wait_recv()
 
-        def across_step(c, _):
+        def across_sum(c):
             total = part[across, tokens, columns(c)] + a_recv[0, t, :, columns(c)].astype(f32)
             c_send[t, :, columns(c)] = total.astype(bf16)
-            return 0
-
-        lax.fori_loop(0, tiles, across_step, 0)
+
+        each_tile(across_sum)
         copy = pltpu.make_async_remote_copy(
             src_ref=c_send.at[t],
             dst_ref=c_recv.at[t],
@@ -388,27 +396,28 @@
         )
         copy.start()
         c_copies[t] = copy
-    for t in range(SUBS):
-        send_partner(1, t, partner)
+
+        def partner_all(c):
+            a_send[1, t, :, columns(c)] = project(partner, t, c, 0, channels).astype(bf16)
+
+        each_tile(partner_all)
+        a_copies[1, t] = to_partner(1, t)
+
+        def own_all(c):
+            part[tp, tokens, columns(c)] = project(tp, t, c, 0, channels)
+
+        each_tile(own_all)
     for t in range(SUBS):
         tokens = pl.ds(t * span, span)
         a_copies[1, t].wait_recv()
-
-        def own_step(c, _):
-            part[tp, tokens, columns(c)] = project(tp, t, c) + a_recv[1, t, :, columns(c)].astype(f32)
-            return 0
-
-        lax.fori_loop(0, tiles, own_step, 0)
-    for t in range(SUBS):
-        tokens = pl.ds(t * span, span)
         c_copies[t].wait_recv()
 
-        def out_step(c, _):
-            total = part[tp, tokens, columns(c)] + c_recv[t, :, columns(c)].astype(f32)
+        def finish(c):
+            total = part[tp, tokens, columns(c)] + a_recv[1, t, :, columns(c)].astype(f32)
+            total = total + c_recv[t, :, columns(c)].astype(f32)
             out[columns(c), tokens] = total.T.astype(bf16)
-            return 0
-
-        lax.fori_loop(0, tiles, out_step, 0)
+
+        each_tile(finish)
     for group in (x_copies, y_copies, a_copies, c_copies):
         for copy in group.values():
             copy.wait_send()
@@ -418,8 +427,8 @@
     channels, width = signal.shape
     n = lax.axis_size("ctx")
     feats = out_weight.shape[1] // 4
-    half = channels // HALVES
-    ch = half // n
+    mine = channels // n
+    most = max(chunk_sizes(mine))
     span = width // SUBS
     vmem = pl.BlockSpec(memory_space=pltpu.VMEM)
     hbm = pl.BlockSpec(memory_space=pl.ANY)
@@ -430,11 +439,11 @@
         in_specs=[vmem] * 5 + [hbm] * 2,
         out_specs=vmem,
         scratch_shapes=[
-            pltpu.VMEM((HALVES, n, 2 * ch, width), bf16),
-            pltpu.VMEM((HALVES, n, 2 * ch, width), bf16),
-            pltpu.VMEM((n + 1, 2 * ch, 2 * width), bf16),
-            pltpu.VMEM((n + 1, ch, 2 * width), f32),
-            pltpu.VMEM((HALVES, SUBS, n, ch, span), bf16),
+            pltpu.VMEM((n, 2 * mine, width), bf16),
+            pltpu.VMEM((n, 2 * mine, width), bf16),
+            pltpu.VMEM((n + 1, 2 * most, 2 * width), bf16),
+            pltpu.VMEM((n + 1, most, 2 * width), f32),
+            pltpu.VMEM((SUBS, n, mine, span), bf16),
             pltpu.VMEM((SUBS, channels, span), bf16),
             pltpu.VMEM((n + 1, 2 * width, 2 * width), bf16),
             pltpu.VMEM((4, channels, feats), bf16),
@@ -445,10 +454,10 @@
             pltpu.VMEM((SUBS, span, feats), bf16),
             pltpu.VMEM((SUBS, span, feats), bf16),
             dma((5,)),
-            dma((HALVES, n)),
-            dma((HALVES, n)),
-            dma((HALVES, SUBS, n)),
-            dma((HALVES, SUBS, n)),
+            dma((CHUNKS, n)),
+            dma((CHUNKS, n)),
+            dma((CHUNKS, SUBS, n)),
+            dma((CHUNKS, SUBS, n)),
             dma((2, SUBS)),
             dma((2, SUBS)),
             dma((SUBS,)),
@@ -468,7 +477,7 @@
     features = rest[-1].shape[1]
     n, tp = lax.axis_size("ctx"), lax.axis_size("tp")
     fits = n in (2, 4, 8) and tp == 4 and width % 256 == 0
-    fits = fits and channels % (HALVES * n * 16) == 0 and channels % (HALVES * 128) == 0
+    fits = fits and channels % (4 * n * 16) == 0 and channels % (4 * 128) == 0
     fits = fits and features % (4 * 256) == 0
     return (per_device_fused if fits else per_device_generic)(signal, *rest)
 

time: 62.9 us -> 63.6 us (1.011)
  Pallas kernels: 60.8 us -> 61.5 us
    pallas_call x1, Pallas kernels: 60.8 us -> 61.5 us  [per_device_fused(): pl.pallas_call(functools.partial(fused_kernel, n), out_shape=jax.ShapeDty...]
where the time goes in v4:
time: 63.6 us; the launch traced here: 63.4 us
  Pallas kernels  61.5 us (97%)
  local copies, waits for them, and re-layouts  1.87 us (3%)
    pallas_call x1, Pallas kernels, per_device_fused(): pl.pallas_call(functools.partial(fused_kernel, n), out_shape=jax.ShapeDty...  61.5 us
    unnamed x1, local copies, waits for them, and re-layouts  1.87 us

profile of v4, /device:TPU:0, one launch (start us, length us, event | category | flops | bytes accessed | tf_op | source)
XLA Modules:
  0.0 63.4 jit_solution(3562546919065546654)
XLA Ops:
  0.0 61.5 %shard_map.73 = bf16[1024,256]{1,0:T(8,128)(2,1)} custom-call(bf16[1024,256]{1,0:T(8,128)(2,1)} %sig.1, bf16[1024,256]{1,0:T(8,128)(2,1)} %pre.1, bf16[1024,256]{1,0:T(8,128)(2,1)} %post.1, f32[1024,256]{1,0:T(8,128)} %taps.1, f32[8,128]{1,0:T(8,128)} %bitcast.1, bf16[1024,4096]{1,0:T(8,128)(2,1)} %weight_hbm.1, bf16[9,512,512]{2,1,0:T(8,128)(2,1)} %constant.2.clone.table_hbm), custom_call_target="tpu_custom_call" | custom-call | tf_op jit(solution)/shard_map/pallas_call | solution.py:436
  61.5 1.9 %copy.9 = bf16[1024,256]{1,0:T(8,128)(2,1)} copy(bf16[1024,256]{1,0:T(8,128)(2,1)} %shard_map.73) | data formatting | bytes 1048576

commit v5 on v4

--- a/solution.py
+++ b/solution.py
@@ -189,7 +189,9 @@
     sizes = chunk_sizes(channels // n)
     offsets = (0, sizes[0])
     feats = out.shape[0]
-    order = sorted(range(1, n), key=lambda m: -(m // 2))
+    far_peers = [m for m in range(1, n) if 2 * m >= n]
+    near_peers = [m for m in range(1, n) if 2 * m < n]
+    order = [m for i, far_peer in enumerate(far_peers) for m in [far_peer] + near_peers[i : i + 1]]
     span = width // SUBS
 
     def peer_of(mask):
@@ -206,9 +208,6 @@
         loads.append(
             pltpu.make_async_copy(weight_hbm.at[:, pl.ds(f * feats, feats)], weight.at[f], load_sem.at[1 + f])
         )
-    for load in loads:
-        load.start()
-
     barrier = pltpu.get_barrier_semaphore()
     for d in range(1, n):
         pl.semaphore_signal(barrier, inc=1, device_id={"ctx": peer_of(d)}, device_id_type=MESH)
@@ -247,6 +246,8 @@
             )
             copy.start()
             x_copies[h, d] = copy
+        for load in loads[:1] if h == 0 else loads[1:]:
+            load.start()
     for h in range(CHUNKS):
         fill(x_recv, me, h, me)
     loads[0].wait()
@@ -303,7 +304,7 @@
             middle(k1, size, False, spec, table, wide)
             return 0
 
-        lax.fori_loop(1, n, middle_step, 0)
+        lax.fori_loop(1, n, middle_step, 0, unroll=True)
 
         def back_step(i, _):
             rows = pl.ds(pl.multiple_of(i * ROWS, ROWS), ROWS)

time: 63.6 us -> 63 us (level)
  no operation moved by 1% of the time
where the time goes in v5:
time: 63 us; the launch traced here: 62.8 us
  Pallas kernels  60.9 us (97%)
  local copies, waits for them, and re-layouts  1.87 us (3%)
    pallas_call x1, Pallas kernels, per_device_fused(): pl.pallas_call(functools.partial(fused_kernel, n), out_shape=jax.ShapeDty...  60.9 us
    unnamed x1, local copies, waits for them, and re-layouts  1.87 us

profile of v5, /device:TPU:0, one launch (start us, length us, event | category | flops | bytes accessed | tf_op | source)
XLA Modules:
  0.0 62.8 jit_solution(5612383517075281220)
XLA Ops:
  0.0 60.9 %shard_map.73 = bf16[1024,256]{1,0:T(8,128)(2,1)} custom-call(bf16[1024,256]{1,0:T(8,128)(2,1)} %sig.1, bf16[1024,256]{1,0:T(8,128)(2,1)} %pre.1, bf16[1024,256]{1,0:T(8,128)(2,1)} %post.1, f32[1024,256]{1,0:T(8,128)} %taps.1, f32[8,128]{1,0:T(8,128)} %bitcast.1, bf16[1024,4096]{1,0:T(8,128)(2,1)} %weight_hbm.1, bf16[9,512,512]{2,1,0:T(8,128)(2,1)} %constant.2.clone.table_hbm), custom_call_target="tpu_custom_call" | custom-call | tf_op jit(solution)/shard_map/pallas_call | solution.py:437
  60.9 1.9 %copy.9 = bf16[1024,256]{1,0:T(8,128)(2,1)} copy(bf16[1024,256]{1,0:T(8,128)(2,1)} %shard_map.73) | data formatting | bytes 1048576

commit v6 on v5

--- a/solution.py
+++ b/solution.py
@@ -169,6 +169,7 @@
 MESH = pl.DeviceIdType.MESH
 CHUNKS = 2
 SUBS = 2
+PIECES = 2
 
 
 def chunk_sizes(mine):
@@ -176,9 +177,9 @@
 
 
 def fused_kernel(
-    n, sig, pre, post, taps, skip, weight_hbm, table_hbm, out,
-    x_send, x_recv, spec, wide, y_send, y_recv, table, weight, mixed_t, part, a_send, a_recv, c_send, c_recv,
-    load_sem, xs_sem, xr_sem, ys_sem, yr_sem, as_sem, ar_sem, cs_sem, cr_sem,
+    n, sig_hbm, pre_hbm, post_hbm, taps_hbm, skip, weight_hbm, table_hbm, out,
+    sig, pre, post, taps, x_send, x_recv, spec, wide, y_send, y_recv, table, weight, mixed_t, part, a_send, a_recv, c_send, c_recv,
+    in_sem, load_sem, xs_sem, xr_sem, ys_sem, yr_sem, as_sem, ar_sem, cs_sem, cr_sem,
 ):
     me = lax.axis_index("ctx")
     tp = lax.axis_index("tp")
@@ -203,6 +204,18 @@
         return peer
 
 
+    in_loads = []
+    for h in range(CHUNKS):
+        rows = pl.ds(n * offsets[h], n * sizes[h])
+        pairs = ((sig_hbm, sig), (pre_hbm, pre), (taps_hbm, taps), (post_hbm, post))
+        in_loads.append(
+            [
+                pltpu.make_async_copy(source.at[rows], target.at[rows], in_sem.at[h, i])
+                for i, (source, target) in enumerate(pairs)
+            ]
+        )
+        for load in in_loads[h][:3]:
+            load.start()
     loads = [pltpu.make_async_copy(table_hbm, table, load_sem.at[0])]
     for f in range(4):
         loads.append(
@@ -231,6 +244,8 @@
 
     x_copies = {}
     for h in range(CHUNKS):
+        for load in in_loads[h][:3]:
+            load.wait()
         for d in order:
             fill(x_send, d, h, peer_of(d))
         if h == 0:
@@ -248,6 +263,7 @@
             x_copies[h, d] = copy
         for load in loads[:1] if h == 0 else loads[1:]:
             load.start()
+        in_loads[h][3].start()
     for h in range(CHUNKS):
         fill(x_recv, me, h, me)
     loads[0].wait()
@@ -323,7 +339,7 @@
         send_back(0, t)
         send_back(1, t)
 
-    for load in loads[1:]:
+    for load in loads[1:] + [in_loads[h][3] for h in range(CHUNKS)]:
         load.wait()
     tile = 256
     tiles = feats // tile
@@ -332,25 +348,25 @@
     def columns(c):
         return pl.ds(pl.multiple_of(c * tile, tile), tile)
 
-    def project(f, t, c, lo, hi):
-        return jnp.dot(
-            mixed_t[t * span : (t + 1) * span, lo:hi], weight[f, lo:hi, columns(c)], preferred_element_type=f32
-        )
-
-    def each_tile(body):
+    def project(f, tokens, c, lo, hi):
+        return jnp.dot(mixed_t[tokens, lo:hi], weight[f, lo:hi, columns(c)], preferred_element_type=f32)
+
+    def each_tile(body, piece=None):
         def step(c, _):
             body(c)
             return 0
 
-        lax.fori_loop(0, tiles, step, 0)
-
-    def to_partner(slot, t):
+        lo, hi = (0, tiles) if piece is None else (piece * tiles // PIECES, (piece + 1) * tiles // PIECES)
+        lax.fori_loop(lo, hi, step, 0)
+
+    def reduce_copy(send, recv, send_sems, recv_sems, at, piece, target):
+        cut = pl.ds(piece * (feats // PIECES), feats // PIECES)
         copy = pltpu.make_async_remote_copy(
-            src_ref=a_send.at[slot, t],
-            dst_ref=a_recv.at[slot, t],
-            send_sem=as_sem.at[slot, t],
-            recv_sem=ar_sem.at[slot, t],
-            device_id={"tp": partner},
+            src_ref=send.at[(*at, slice(None), cut)],
+            dst_ref=recv.at[(*at, slice(None), cut)],
+            send_sem=send_sems.at[(*at, piece)],
+            recv_sem=recv_sems.at[(*at, piece)],
+            device_id={"tp": target},
             device_id_type=MESH,
         )
         copy.start()
@@ -363,62 +379,67 @@
         mix(0, t)
 
         def early(c):
-            part[far, tokens, columns(c)] = project(far, t, c, 0, head)
-            part[across, tokens, columns(c)] = project(across, t, c, 0, head)
+            part[far, tokens, columns(c)] = project(far, tokens, c, 0, head)
+            part[across, tokens, columns(c)] = project(across, tokens, c, 0, head)
 
         each_tile(early)
         mix(1, t)
 
         def far_rest(c):
-            total = part[far, tokens, columns(c)] + project(far, t, c, head, channels)
+            total = part[far, tokens, columns(c)] + project(far, tokens, c, head, channels)
             a_send[0, t, :, columns(c)] = total.astype(bf16)
 
-        each_tile(far_rest)
-        a_copies[0, t] = to_partner(0, t)
+        for piece in range(PIECES):
+            each_tile(far_rest, piece)
+            a_copies[0, t, piece] = reduce_copy(a_send, a_recv, as_sem, ar_sem, (0, t), piece, partner)
 
         def across_rest(c):
-            part[across, tokens, columns(c)] += project(across, t, c, head, channels)
+            part[across, tokens, columns(c)] += project(across, tokens, c, head, channels)
 
         each_tile(across_rest)
-        a_copies[0, t].wait_recv()
 
         def across_sum(c):
             total = part[across, tokens, columns(c)] + a_recv[0, t, :, columns(c)].astype(f32)
             c_send[t, :, columns(c)] = total.astype(bf16)
 
-        each_tile(across_sum)
-        copy = pltpu.make_async_remote_copy(
-            src_ref=c_send.at[t],
-            dst_ref=c_recv.at[t],
-            send_sem=cs_sem.at[t],
-            recv_sem=cr_sem.at[t],
-            device_id={"tp": across},
-            device_id_type=MESH,
-        )
-        copy.start()
-        c_copies[t] = copy
-
-        def partner_all(c):
-            a_send[1, t, :, columns(c)] = project(partner, t, c, 0, channels).astype(bf16)
-
-        each_tile(partner_all)
-        a_copies[1, t] = to_partner(1, t)
-
-        def own_all(c):
-            part[tp, tokens, columns(c)] = project(tp, t, c, 0, channels)
-
-        each_tile(own_all)
+        for piece in range(PIECES):
+            a_copies[0, t, piece].wait_recv()
+            each_tile(across_sum, piece)
+            c_copies[t, piece] = reduce_copy(c_send, c_recv, cs_sem, cr_sem, (t,), piece, across)
+
+    def partner_all(c):
+        total = project(partner, pl.ds(0, width), c, 0, channels).astype(bf16)
+        for t in range(SUBS):
+            a_send[1, t, :, columns(c)] = total[t * span : (t + 1) * span]
+
+    for piece in range(PIECES):
+        each_tile(partner_all, piece)
+        for t in range(SUBS):
+            a_copies[1, t, piece] = reduce_copy(a_send, a_recv, as_sem, ar_sem, (1, t), piece, partner)
+
+    def own_all(c):
+        part[tp, :, columns(c)] = project(tp, pl.ds(0, width), c, 0, channels)
+
+    each_tile(own_all)
+    for t in range(SUBS):
+        for piece in range(PIECES):
+            a_copies[1, t, piece].wait_recv()
+        tokens = pl.ds(t * span, span)
+
+        def own_sum(c):
+            part[tp, tokens, columns(c)] += a_recv[1, t, :, columns(c)].astype(f32)
+
+        each_tile(own_sum)
     for t in range(SUBS):
         tokens = pl.ds(t * span, span)
-        a_copies[1, t].wait_recv()
-        c_copies[t].wait_recv()
 
         def finish(c):
-            total = part[tp, tokens, columns(c)] + a_recv[1, t, :, columns(c)].astype(f32)
-            total = total + c_recv[t, :, columns(c)].astype(f32)
+            total = part[tp, tokens, columns(c)] + c_recv[t, :, columns(c)].astype(f32)
             out[columns(c), tokens] = total.T.astype(bf16)
 
-        each_tile(finish)
+        for piece in range(PIECES):
+            c_copies[t, piece].wait_recv()
+            each_tile(finish, piece)
     for group in (x_copies, y_copies, a_copies, c_copies):
         for copy in group.values():
             copy.wait_send()
@@ -437,9 +458,13 @@
     return pl.pallas_call(
         functools.partial(fused_kernel, n),
         out_shape=jax.ShapeDtypeStruct((feats, width), bf16),
-        in_specs=[vmem] * 5 + [hbm] * 2,
+        in_specs=[hbm] * 4 + [vmem] + [hbm] * 2,
         out_specs=vmem,
         scratch_shapes=[
+            pltpu.VMEM((channels, width), bf16),
+            pltpu.VMEM((channels, width), bf16),
+            pltpu.VMEM((channels, width), bf16),
+            pltpu.VMEM((channels, width), f32),
             pltpu.VMEM((n, 2 * mine, width), bf16),
             pltpu.VMEM((n, 2 * mine, width), bf16),
             pltpu.VMEM((n + 1, 2 * most, 2 * width), bf16),
@@ -454,15 +479,16 @@
             pltpu.VMEM((2, SUBS, span, feats), bf16),
             pltpu.VMEM((SUBS, span, feats), bf16),
             pltpu.VMEM((SUBS, span, feats), bf16),
+            dma((CHUNKS, 4)),
             dma((5,)),
             dma((CHUNKS, n)),
             dma((CHUNKS, n)),
             dma((CHUNKS, SUBS, n)),
             dma((CHUNKS, SUBS, n)),
-            dma((2, SUBS)),
-            dma((2, SUBS)),
-            dma((SUBS,)),
-            dma((SUBS,)),
+            dma((2, SUBS, PIECES)),
+            dma((2, SUBS, PIECES)),
+            dma((SUBS, PIECES)),
+            dma((SUBS, PIECES)),
         ],
         compiler_params=pltpu.CompilerParams(
             collective_id=0, has_side_effects=True, vmem_limit_bytes=56 * 1024 * 1024
@@ -479,7 +505,7 @@
     n, tp = lax.axis_size("ctx"), lax.axis_size("tp")
     fits = n in (2, 4, 8) and tp == 4 and width % 256 == 0
     fits = fits and channels % (4 * n * 16) == 0 and channels % (4 * 128) == 0
-    fits = fits and features % (4 * 256) == 0
+    fits = fits and features % (4 * PIECES * 256) == 0
     return (per_device_fused if fits else per_device_generic)(signal, *rest)
 
 

time: 63 us -> 61.6 us (0.978)
  Pallas kernels: 60.9 us -> 59.5 us
    pallas_call x1, Pallas kernels: 60.9 us -> 59.5 us  [per_device_fused(): pl.pallas_call(functools.partial(fused_kernel, n), out_shape=jax.ShapeDty...]
where the time goes in v6:
time: 61.6 us; the launch traced here: 61.4 us
  Pallas kernels  59.5 us (97%)
  local copies, waits for them, and re-layouts  1.87 us (3%)
    pallas_call x1, Pallas kernels, per_device_fused(): pl.pallas_call(functools.partial(fused_kernel, n), out_shape=jax.ShapeDty...  59.5 us
    unnamed x1, local copies, waits for them, and re-layouts  1.87 us

profile of v6, /device:TPU:0, one launch (start us, length us, event | category | flops | bytes accessed | tf_op | source)
XLA Modules:
  0.0 61.4 jit_solution(16338327940435960490)
XLA Ops:
  0.0 59.5 %shard_map.73 = bf16[1024,256]{1,0:T(8,128)(2,1)} custom-call(bf16[1024,256]{1,0:T(8,128)(2,1)} %sig_hbm.1, bf16[1024,256]{1,0:T(8,128)(2,1)} %pre_hbm.1, bf16[1024,256]{1,0:T(8,128)(2,1)} %post_hbm.1, f32[1024,256]{1,0:T(8,128)} %taps_hbm.1, f32[8,128]{1,0:T(8,128)} %bitcast.1, bf16[1024,4096]{1,0:T(8,128)(2,1)} %weight_hbm.1, ...), custom_call_target="tpu_custom_call" | custom-call | tf_op jit(solution)/shard_map/pallas_call | solution.py:458
  59.5 1.9 %copy.9 = bf16[1024,256]{1,0:T(8,128)(2,1)} copy(bf16[1024,256]{1,0:T(8,128)(2,1)} %shard_map.73) | data formatting | bytes 1048576

commit v7 on v6

--- a/solution.py
+++ b/solution.py
@@ -177,9 +177,9 @@
 
 
 def fused_kernel(
-    n, sig_hbm, pre_hbm, post_hbm, taps_hbm, skip, weight_hbm, table_hbm, out,
-    sig, pre, post, taps, x_send, x_recv, spec, wide, y_send, y_recv, table, weight, mixed_t, part, a_send, a_recv, c_send, c_recv,
-    in_sem, load_sem, xs_sem, xr_sem, ys_sem, yr_sem, as_sem, ar_sem, cs_sem, cr_sem,
+    n, sig_hbm, pre_hbm, post_hbm, taps_hbm, skip, weight_hbm, table_hbm, out_any,
+    out, sig, pre, post, taps, x_send, x_recv, spec, wide, y_send, y_recv, table, weight, mixed_t, part, a_send, a_recv, c_send, c_recv,
+    out_sem, in_sem, load_sem, xs_sem, xr_sem, ys_sem, yr_sem, as_sem, ar_sem, cs_sem, cr_sem,
 ):
     me = lax.axis_index("ctx")
     tp = lax.axis_index("tp")
@@ -372,7 +372,7 @@
         copy.start()
         return copy
 
-    a_copies, c_copies = {}, {}
+    a_copies, c_copies, out_copies = {}, {}, []
     far = (1 - row) * 2 + (1 - core)
     for t in range(SUBS):
         tokens = pl.ds(t * span, span)
@@ -440,6 +440,12 @@
         for piece in range(PIECES):
             c_copies[t, piece].wait_recv()
             each_tile(finish, piece)
+            rows = pl.ds(piece * (feats // PIECES), feats // PIECES)
+            copy = pltpu.make_async_copy(out.at[rows, tokens], out_any.at[rows, tokens], out_sem.at[t, piece])
+            copy.start()
+            out_copies.append(copy)
+    for copy in out_copies:
+        copy.wait()
     for group in (x_copies, y_copies, a_copies, c_copies):
         for copy in group.values():
             copy.wait_send()
@@ -453,14 +459,15 @@
     most = max(chunk_sizes(mine))
     span = width // SUBS
     vmem = pl.BlockSpec(memory_space=pltpu.VMEM)
-    hbm = pl.BlockSpec(memory_space=pl.ANY)
+    hbm = pl.BlockSpec(memory_space=pltpu.HBM)
     dma = pltpu.SemaphoreType.DMA
     return pl.pallas_call(
         functools.partial(fused_kernel, n),
         out_shape=jax.ShapeDtypeStruct((feats, width), bf16),
         in_specs=[hbm] * 4 + [vmem] + [hbm] * 2,
-        out_specs=vmem,
+        out_specs=pl.BlockSpec(memory_space=pl.ANY),
         scratch_shapes=[
+            pltpu.VMEM((feats, width), bf16),
             pltpu.VMEM((channels, width), bf16),
             pltpu.VMEM((channels, width), bf16),
             pltpu.VMEM((channels, width), bf16),
@@ -479,6 +486,7 @@
             pltpu.VMEM((2, SUBS, span, feats), bf16),
             pltpu.VMEM((SUBS, span, feats), bf16),
             pltpu.VMEM((SUBS, span, feats), bf16),
+            dma((SUBS, PIECES)),
             dma((CHUNKS, 4)),
             dma((5,)),
             dma((CHUNKS, n)),
@@ -491,7 +499,7 @@
             dma((SUBS, PIECES)),
         ],
         compiler_params=pltpu.CompilerParams(
-            collective_id=0, has_side_effects=True, vmem_limit_bytes=56 * 1024 * 1024
+            collective_id=0, has_side_effects=True, vmem_limit_bytes=40 * 1024 * 1024
         ),
     )(
         signal, pre_gate, post_gate, filter_taps, skip_gain.reshape(channels // 128, 128), out_weight,

time: 61.6 us -> 67.5 us (1.096)
  local copies, waits for them, and re-layouts: 1.87 us -> 8.17 us
    unnamed x1 -> x13, local copies, waits for them, and re-layouts: 1.87 us -> 8.17 us
where the time goes in v7:
time: 67.5 us; the launch traced here: 67.1 us
  Pallas kernels  58.9 us (87%)
  local copies, waits for them, and re-layouts  8.17 us (12%)
    pallas_call x1, Pallas kernels, per_device_fused(): pl.pallas_call(functools.partial(fused_kernel, n), out_shape=jax.ShapeDty...  58.9 us
    unnamed x13, local copies, waits for them, and re-layouts  8.17 us

profile of v7, /device:TPU:0, one launch (start us, length us, event | category | flops | bytes accessed | tf_op | source)
XLA Modules:
  0.0 67.1 jit_solution(2777582103211871739)
XLA Ops:
  0.0 0.0 copy-start
  0.0 2.3 %copy-done = bf16[9,512,512]{2,1,0:T(8,128)(2,1)S(1)} copy-done((bf16[9,512,512]{2,1,0:T(8,128)(2,1)S(1)}, bf16[9,512,512]{2,1,0:T(8,128)(2,1)}, u32[]{:S(2)}) %copy-start) | copy-done | bytes 4718616
  2.3 0.0 copy-start.1
  2.3 1.2 %copy-done.1 = f32[1024,256]{1,0:T(8,128)S(1)} copy-done((f32[1024,256]{1,0:T(8,128)S(1)}, f32[1024,256]{1,0:T(8,128)}, u32[]{:S(2)}) %copy-start.1) | copy-done | bytes 1048600
  3.6 0.0 copy-start.2
  3.6 1.0 %copy-done.2 = bf16[1024,256]{1,0:T(8,128)(2,1)S(1)} copy-done((bf16[1024,256]{1,0:T(8,128)(2,1)S(1)}, bf16[1024,256]{1,0:T(8,128)(2,1)}, u32[]{:S(2)}) %copy-start.2) | copy-done | bytes 524312
  4.6 0.0 copy-start.3
  4.6 1.0 %copy-done.3 = bf16[1024,256]{1,0:T(8,128)(2,1)S(1)} copy-done((bf16[1024,256]{1,0:T(8,128)(2,1)S(1)}, bf16[1024,256]{1,0:T(8,128)(2,1)}, u32[]{:S(2)}) %copy-start.3) | copy-done | bytes 524312
  5.6 0.0 copy-start.4
  5.6 1.0 %copy-done.4 = bf16[1024,256]{1,0:T(8,128)(2,1)S(1)} copy-done((bf16[1024,256]{1,0:T(8,128)(2,1)S(1)}, bf16[1024,256]{1,0:T(8,128)(2,1)}, u32[]{:S(2)}) %copy-start.4) | copy-done | bytes 524312
  6.7 0.0 copy-start.5
  6.7 0.7 %copy-done.5 = f32[1024]{0:T(1024)S(1)} copy-done((f32[1024]{0:T(1024)S(1)}, f32[1024]{0:T(1024)}, u32[]{:S(2)}) %copy-start.5) | copy-done | bytes 4120
  7.4 58.9 %shard_map.73 = bf16[1024,256]{1,0:T(8,128)(2,1)S(1)} custom-call(bf16[1024,256]{1,0:T(8,128)(2,1)S(1)} %copy-done.2, bf16[1024,256]{1,0:T(8,128)(2,1)S(1)} %copy-done.3, bf16[1024,256]{1,0:T(8,128)(2,1)S(1)} %copy-done.4, f32[1024,256]{1,0:T(8,128)S(1)} %copy-done.1, f32[8,128]{1,0:T(8,128)S(1)} %bitcast.1, bf16[1024,4096]{1,0:T(8,128)(2,1)} %weight_hbm.1, ...), custom_call_target="tpu_custom_call" | custom-call | tf_op jit(solution)/shard_map/pallas_call | solution.py:464
  66.3 0.8 %copy.9 = bf16[1024,256]{1,0:T(8,128)(2,1)} copy(bf16[1024,256]{1,0:T(8,128)(2,1)S(1)} %shard_map.73) | data formatting | bytes 1048576
Async XLA Ops:
  0.0 2.3 %copy-start = (bf16[9,512,512]{2,1,0:T(8,128)(2,1)S(1)}, bf16[9,512,512]{2,1,0:T(8,128)(2,1)}, u32[]{:S(2)}) copy-start(bf16[9,512,512]{2,1,0:T(8,128)(2,1)} %constant.2.clone.table_hbm) | copy-start | bytes 14155780
  2.3 1.2 %copy-start.1 = (f32[1024,256]{1,0:T(8,128)S(1)}, f32[1024,256]{1,0:T(8,128)}, u32[]{:S(2)}) copy-start(f32[1024,256]{1,0:T(8,128)} %taps_hbm.1) | copy-start | bytes 3145732
  3.6 1.0 %copy-start.2 = (bf16[1024,256]{1,0:T(8,128)(2,1)S(1)}, bf16[1024,256]{1,0:T(8,128)(2,1)}, u32[]{:S(2)}) copy-start(bf16[1024,256]{1,0:T(8,128)(2,1)} %sig_hbm.1) | copy-start | bytes 1572868
  4.6 1.0 %copy-start.3 = (bf16[1024,256]{1,0:T(8,128)(2,1)S(1)}, bf16[1024,256]{1,0:T(8,128)(2,1)}, u32[]{:S(2)}) copy-start(bf16[1024,256]{1,0:T(8,128)(2,1)} %pre_hbm.1) | copy-start | bytes 1572868
  5.6 1.0 %copy-start.4 = (bf16[1024,256]{1,0:T(8,128)(2,1)S(1)}, bf16[1024,256]{1,0:T(8,128)(2,1)}, u32[]{:S(2)}) copy-start(bf16[1024,256]{1,0:T(8,128)(2,1)} %post_hbm.1) | copy-start | bytes 1572868
  6.7 0.7 %copy-start.5 = (f32[1024]{0:T(1024)S(1)}, f32[1024]{0:T(1024)}, u32[]{:S(2)}) copy-start(f32[1024]{0:T(1024)} %param.11) | copy-start | bytes 12292

commit v8 on v7

--- a/solution.py
+++ b/solution.py
@@ -499,7 +499,7 @@
             dma((SUBS, PIECES)),
         ],
         compiler_params=pltpu.CompilerParams(
-            collective_id=0, has_side_effects=True, vmem_limit_bytes=40 * 1024 * 1024
+            collective_id=0, has_side_effects=True, vmem_limit_bytes=56 * 1024 * 1024
         ),
     )(
         signal, pre_gate, post_gate, filter_taps, skip_gain.reshape(channels // 128, 128), out_weight,

time: 67.5 us -> 61.5 us (0.911)
  local copies, waits for them, and re-layouts: 8.17 us -> 1.87 us
    unnamed x13 -> x1, local copies, waits for them, and re-layouts: 8.17 us -> 1.87 us
where the time goes in v8:
time: 61.5 us; the launch traced here: 61.3 us
  Pallas kernels  59.4 us (97%)
  local copies, waits for them, and re-layouts  1.87 us (3%)
    pallas_call x1, Pallas kernels, per_device_fused(): pl.pallas_call(functools.partial(fused_kernel, n), out_shape=jax.ShapeDty...  59.4 us
    unnamed x1, local copies, waits for them, and re-layouts  1.87 us

profile of v8, /device:TPU:0, one launch (start us, length us, event | category | flops | bytes accessed | tf_op | source)
XLA Modules:
  0.0 61.3 jit_solution(10010082913527298143)
XLA Ops:
  0.0 59.4 %shard_map.73 = bf16[1024,256]{1,0:T(8,128)(2,1)} custom-call(bf16[1024,256]{1,0:T(8,128)(2,1)} %sig_hbm.1, bf16[1024,256]{1,0:T(8,128)(2,1)} %pre_hbm.1, bf16[1024,256]{1,0:T(8,128)(2,1)} %post_hbm.1, f32[1024,256]{1,0:T(8,128)} %taps_hbm.1, f32[8,128]{1,0:T(8,128)} %bitcast.1, bf16[1024,4096]{1,0:T(8,128)(2,1)} %weight_hbm.1, ...), custom_call_target="tpu_custom_call" | custom-call | tf_op jit(solution)/shard_map/pallas_call | solution.py:464
  59.4 1.9 %copy.9 = bf16[1024,256]{1,0:T(8,128)(2,1)} copy(bf16[1024,256]{1,0:T(8,128)(2,1)} %shard_map.73) | data formatting | bytes 1048576
